TPU v7x, 256 devices: a whole 4x4x8 slice. The times are simulated.
256 devices in a mesh: src: 8 (over z), tgt: 32 (over y, x, core).
Axes of the slice: x: 4, y: 4, z: 8, core: 2. Of those that a mesh axis runs over, the one named last changes fastest.
Arguments:
- source_latent: bfloat16 [64, 32768], P(None, 'src'), may hold values from -14 to 14
- target_latent: bfloat16 [64, 32768], P(None, 'tgt'), may hold values from -14 to 14
- source_mass: float32 [32768], P('src'), may hold values from 0.25 to 4
- target_mass: float32 [32768], P('tgt'), may hold values from 0.25 to 4
- source_region: int32 [32], P('src'), may hold values from 0 to 15, as said below
- target_region: int32 [64], P('tgt'), may hold values from 0 to 15, as said below
- allowed: int32 [16, 16], replicated, may hold values from 0 to 1, as said below
Outputs:
- source_potential: float32 [32768], P('src')
- target_potential: float32 [32768], P('tgt')
- projected: float32 [64, 32768], P('src', 'tgt')
Inputs may be any that keep to these rules, and one draw needn't show every extreme that they name: `source_region`: every one of the 16 regions labels at least one source block. `target_region`: every one of the 16 regions labels at least one target block. `allowed`: the diagonal is 1.
All inputs are finite; a program needn't handle non-finite values.
Results may differ from a plain program's by a relative error of at most 0.0022.
Values sent between devices are 32-bit elements; how exact they have to be, the bound alone decides.
A program may use at most 64 MiB of HBM per device.

v0:
```python
import jax
import jax.numpy as jnp
from jax import lax
from jax.sharding import PartitionSpec as P

SB = 1024
TB = 512
ITERS = 3


ENTROPIC = 0.05
MARGINAL = 1.0
DAMPING = MARGINAL / (MARGINAL + ENTROPIC)
NEGATIVE = -1e30


def join_pairs(first, second):
    largest = jnp.maximum(first[0], second[0])
    summed = first[1] * jnp.exp(first[0] - largest) + second[1] * jnp.exp(second[0] - largest)
    return (largest, summed)


def tile_distance(source_latent, source_square, target_latent, target_square, row_block, col_block):
    source_block = lax.dynamic_slice_in_dim(source_latent, row_block * SB, SB, 1)
    target_block = lax.dynamic_slice_in_dim(target_latent, col_block * TB, TB, 1)
    products = lax.dot_general(
        source_block, target_block, (((0,), (0,)), ((), ())), preferred_element_type=jnp.float32
    )
    source_part = lax.dynamic_slice_in_dim(source_square, row_block * SB, SB, 0)
    target_part = lax.dynamic_slice_in_dim(target_square, col_block * TB, TB, 0)
    return (source_part[:, None] + target_part[None, :] - 2.0 * products) / source_latent.shape[0]


def row_reduce(largest, summed):
    whole_max = lax.pmax(largest, "tgt")
    summed = lax.psum(summed * jnp.exp(largest - whole_max), "tgt")
    largest = whole_max
    return largest + jnp.log(summed)


def col_reduce(largest, summed):
    whole_max = lax.pmax(largest, "src")
    summed = lax.psum(summed * jnp.exp(largest - whole_max), "src")
    largest = whole_max
    return largest + jnp.log(summed)


def per_device(
    source_latent, target_latent, source_mass, target_mass, source_region, target_region, allowed
):
    width = source_latent.shape[0]
    source_cells = source_latent.shape[1]
    target_cells = target_latent.shape[1]
    row_blocks = source_cells // SB
    col_blocks = target_cells // TB
    tiles = row_blocks * col_blocks
    source_wide = source_latent.astype(jnp.float32)
    target_wide = target_latent.astype(jnp.float32)
    source_square = jnp.sum(source_wide * source_wide, axis=0)
    target_square = jnp.sum(target_wide * target_wide, axis=0)
    source_log = jnp.log(source_mass)
    target_log = jnp.log(target_mass)
    labels = jnp.arange(allowed.shape[0], dtype=jnp.int32)
    row_hot = (source_region[:, None] == labels[None, :]).astype(jnp.float32)
    col_hot = (target_region[:, None] == labels[None, :]).astype(jnp.float32)
    tile_allowed = jnp.dot(jnp.dot(row_hot, allowed.astype(jnp.float32)), col_hot.T) > 0.5

    def tile_pair(compute, permitted):
        largest, summed = compute(0)
        return (jnp.where(permitted, largest, NEGATIVE), jnp.where(permitted, summed, 0.0))

    potential_target = jnp.zeros((target_cells,), jnp.float32)
    potential_source = jnp.zeros((source_cells,), jnp.float32)
    col_lse = jnp.zeros((target_cells,), jnp.float32)
    for sweep_index in range(ITERS):

        def row_visit(position, carry):
            maxima, totals = carry
            row_block = position // col_blocks
            col_block = position % col_blocks

            def compute(operand):
                distance = tile_distance(
                    source_latent, source_square, target_latent, target_square, row_block, col_block
                )
                potential = lax.dynamic_slice_in_dim(potential_target, col_block * TB, TB, 0)
                weight_log = lax.dynamic_slice_in_dim(target_log, col_block * TB, TB, 0)
                scores = weight_log[None, :] + (potential[None, :] - distance) / ENTROPIC
                largest = jnp.max(scores, axis=1)
                return (largest, jnp.sum(jnp.exp(scores - largest[:, None]), axis=1))

            fresh = tile_pair(compute, tile_allowed[row_block, col_block])
            before = (
                lax.dynamic_slice_in_dim(maxima, row_block * SB, SB, 0),
                lax.dynamic_slice_in_dim(totals, row_block * SB, SB, 0),
            )
            joined = join_pairs(before, fresh)
            maxima = lax.dynamic_update_slice_in_dim(maxima, joined[0], row_block * SB, 0)
            totals = lax.dynamic_update_slice_in_dim(totals, joined[1], row_block * SB, 0)
            return (maxima, totals)

        row_start = (
            jnp.full((source_cells,), NEGATIVE, jnp.float32),
            jnp.zeros((source_cells,), jnp.float32),
        )
        maxima, totals = lax.fori_loop(0, tiles, row_visit, row_start)
        potential_source = -DAMPING * ENTROPIC * row_reduce(maxima, totals)

        def col_visit(position, carry):
            maxima, totals = carry
            row_block = position // col_blocks
            col_block = position % col_blocks

            def compute(operand):
                distance = tile_distance(
                    source_latent, source_square, target_latent, target_square, row_block, col_block
                )
                potential = lax.dynamic_slice_in_dim(potential_source, row_block * SB, SB, 0)
                weight_log = lax.dynamic_slice_in_dim(source_log, row_block * SB, SB, 0)
                scores = weight_log[:, None] + (potential[:, None] - distance) / ENTROPIC
                largest = jnp.max(scores, axis=0)
                return (largest, jnp.sum(jnp.exp(scores - largest[None, :]), axis=0))

            fresh = tile_pair(compute, tile_allowed[row_block, col_block])
            before = (
                lax.dynamic_slice_in_dim(maxima, col_block * TB, TB, 0),
                lax.dynamic_slice_in_dim(totals, col_block * TB, TB, 0),
            )
            joined = join_pairs(before, fresh)
            maxima = lax.dynamic_update_slice_in_dim(maxima, joined[0], col_block * TB, 0)
            totals = lax.dynamic_update_slice_in_dim(totals, joined[1], col_block * TB, 0)
            return (maxima, totals)

        start = (
            jnp.full((target_cells,), NEGATIVE, jnp.float32),
            jnp.zeros((target_cells,), jnp.float32),
        )
        maxima, totals = lax.fori_loop(0, tiles, col_visit, start)
        col_lse = col_reduce(maxima, totals)
        potential_target = -DAMPING * ENTROPIC * col_lse

    def centre_visit(position, numerator):
        row_block = position // col_blocks
        col_block = position % col_blocks

        def compute(operand):
            distance = tile_distance(
                source_latent, source_square, target_latent, target_square, row_block, col_block
            )
            potential = lax.dynamic_slice_in_dim(potential_source, row_block * SB, SB, 0)
            weight_log = lax.dynamic_slice_in_dim(source_log, row_block * SB, SB, 0)
            lse_part = lax.dynamic_slice_in_dim(col_lse, col_block * TB, TB, 0)
            scores = weight_log[:, None] + (potential[:, None] - distance) / ENTROPIC
            weights = jnp.exp(scores - lse_part[None, :]).astype(jnp.bfloat16)
            source_part = lax.dynamic_slice_in_dim(source_latent, row_block * SB, SB, 1)
            return lax.dot_general(
                source_part, weights, (((1,), (0,)), ((), ())), preferred_element_type=jnp.float32
            )

        permitted = tile_allowed[row_block, col_block]
        fresh = jnp.where(permitted, compute(0), 0.0)
        before = lax.dynamic_slice_in_dim(numerator, col_block * TB, TB, 1)
        return lax.dynamic_update_slice_in_dim(numerator, before + fresh, col_block * TB, 1)

    numerator = lax.fori_loop(0, tiles, centre_visit, jnp.zeros((width, target_cells), jnp.float32))
    summed_all = lax.psum(numerator, "src")
    share = width // lax.axis_size("src")
    projected = lax.dynamic_slice_in_dim(summed_all, lax.axis_index("src") * share, share, 0)
    return (potential_source, potential_target, projected)


def solution(mesh):
    placed = (P(None, "src"), P(None, "tgt"), P("src"), P("tgt"), P("src"), P("tgt"), P())
    return jax.shard_map(
        per_device,
        mesh=mesh,
        in_specs=placed,
        out_specs=(P("src"), P("tgt"), P("src", "tgt")),
        check_vma=False,
    )
```

profile of v0, /device:TPU:2, one launch (start us, length us, event | category | flops | bytes accessed | tf_op | source)
XLA Modules:
  0.0 1131.0 jit_solution(7907273144733152168)
XLA Ops:
  11.1 27.5 %while.117 = (s32[]{:T(128)}, f32[4096]{0:T(1024)S(1)}, f32[4096]{0:T(1024)S(1)}, pred[4,2]{1,0:T(4,128)(4,1)S(1)}, f32[1024]{0:T(1024)S(1)}, /*index=5*/f32[409...) while((s32[]{:T(128)}, f32[4096]{0:T(1024)S(1)}, ...), condition=%wide.region_5.6_spmd, body=%wide.region_2.5_spmd.sunk | while | flops 72357912 | bytes 4452815 | solution.py:106
  38.7 123.3 %pmax.42 = f32[4096]{0:T(1024)S(1)} all-reduce(f32[4096]{0:T(1024)S(1)} %get-tuple-element.1702), channel_id=1, replica_groups=mesh['src'=8,'tgt'=32] {'tgt'}, use_global_device_ids=true, to_apply=%region_6.7 | all-reduce | flops 4096 | bytes 32768 | tf_op jit(solution)/shard_map/pmax | solution.py:35
  162.0 123.8 %psum.49 = f32[4096]{0:T(1024)S(1)} all-reduce(f32[4096]{0:T(1024)S(1)} %exponential_multiply_fusion.2), channel_id=1, replica_groups=mesh['src'=8,'tgt'=32] {'tgt'}, use_global_device_ids=true, to_apply=%region_7.8 | all-reduce | flops 4096 | bytes 32768 | tf_op jit(solution)/shard_map/psum | solution.py:36
  285.8 29.8 %while.118 = (s32[]{:T(128)}, f32[1024]{0:T(1024)S(1)}, f32[1024]{0:T(1024)S(1)}, pred[4,2]{1,0:T(4,128)(4,1)S(1)}, f32[4096]{0:T(1024)S(1)}, /*index=5*/f32[409...) while((s32[]{:T(128)}, f32[1024]{0:T(1024)S(1)}, ...), condition=%wide.region_11.12_spmd, body=%wide.region_8.11_spmd.sunk | while | flops 72354840 | bytes 4452827 | solution.py:138
  293.5 1.7 fusion.69
  315.7 20.0 %pmax.43 = f32[1024]{0:T(1024)S(1)} all-reduce(f32[1024]{0:T(1024)S(1)} %get-tuple-element.1704), channel_id=1, replica_groups=mesh['src'=8,'tgt'=32] {'src'}, use_global_device_ids=true, to_apply=%region_12.13 | all-reduce | flops 1024 | bytes 8192 | tf_op jit(solution)/shard_map/pmax | solution.py:42
  335.7 14.2 %psum.50 = f32[1024]{0:T(1024)S(1)} all-reduce(f32[1024]{0:T(1024)S(1)} %exponential_multiply_fusion.5), channel_id=1, replica_groups=mesh['src'=8,'tgt'=32] {'src'}, use_global_device_ids=true, to_apply=%region_13.14 | all-reduce | flops 1024 | bytes 8192 | tf_op jit(solution)/shard_map/psum | solution.py:43
  349.9 28.4 %while.119 = (s32[]{:T(128)}, f32[4096]{0:T(1024)S(1)}, f32[4096]{0:T(1024)S(1)}, pred[4,2]{1,0:T(4,128)(4,1)S(1)}, f32[1024]{0:T(1024)S(1)}, /*index=5*/f32[102...) while((s32[]{:T(128)}, f32[4096]{0:T(1024)S(1)}, ...), condition=%wide.region_17.18_spmd, body=%wide.region_14.17_spmd.sunk | while | flops 72357912 | bytes 4458971 | solution.py:106
  378.3 123.8 %pmax.44 = f32[4096]{0:T(1024)S(1)} all-reduce(f32[4096]{0:T(1024)S(1)} %get-tuple-element.1706), channel_id=1, replica_groups=mesh['src'=8,'tgt'=32] {'tgt'}, use_global_device_ids=true, to_apply=%region_18.19 | all-reduce | flops 4096 | bytes 32768 | tf_op jit(solution)/shard_map/pmax | solution.py:35
  502.1 123.8 %psum.51 = f32[4096]{0:T(1024)S(1)} all-reduce(f32[4096]{0:T(1024)S(1)} %exponential_multiply_fusion.1), channel_id=1, replica_groups=mesh['src'=8,'tgt'=32] {'tgt'}, use_global_device_ids=true, to_apply=%region_19.20 | all-reduce | flops 4096 | bytes 32768 | tf_op jit(solution)/shard_map/psum | solution.py:36
  625.9 28.7 %while.120 = (s32[]{:T(128)}, f32[1024]{0:T(1024)S(1)}, f32[1024]{0:T(1024)S(1)}, pred[4,2]{1,0:T(4,128)(4,1)S(1)}, f32[4096]{0:T(1024)S(1)}, /*index=5*/f32[409...) while((s32[]{:T(128)}, f32[1024]{0:T(1024)S(1)}, ...), condition=%wide.region_23.24_spmd, body=%wide.region_20.23_spmd.sunk | while | flops 72354840 | bytes 4452827 | solution.py:138
  629.6 1.7 fusion.71
  654.6 16.2 %pmax.45 = f32[1024]{0:T(1024)S(1)} all-reduce(f32[1024]{0:T(1024)S(1)} %get-tuple-element.1708), channel_id=1, replica_groups=mesh['src'=8,'tgt'=32] {'src'}, use_global_device_ids=true, to_apply=%region_24.25 | all-reduce | flops 1024 | bytes 8192 | tf_op jit(solution)/shard_map/pmax | solution.py:42
  670.7 14.2 %psum.52 = f32[1024]{0:T(1024)S(1)} all-reduce(f32[1024]{0:T(1024)S(1)} %exponential_multiply_fusion.4), channel_id=1, replica_groups=mesh['src'=8,'tgt'=32] {'src'}, use_global_device_ids=true, to_apply=%region_25.26 | all-reduce | flops 1024 | bytes 8192 | tf_op jit(solution)/shard_map/psum | solution.py:43
  685.0 29.3 %while.121 = (s32[]{:T(128)}, f32[4096]{0:T(1024)S(1)}, f32[4096]{0:T(1024)S(1)}, pred[4,2]{1,0:T(4,128)(4,1)S(1)}, f32[1024]{0:T(1024)S(1)}, /*index=5*/f32[102...) while((s32[]{:T(128)}, f32[4096]{0:T(1024)S(1)}, ...), condition=%wide.region_29.30_spmd, body=%wide.region_26.29_spmd.sunk | while | flops 72357912 | bytes 4458971 | solution.py:106
  714.2 123.7 %pmax.46 = f32[4096]{0:T(1024)S(1)} all-reduce(f32[4096]{0:T(1024)S(1)} %get-tuple-element.1710), channel_id=1, replica_groups=mesh['src'=8,'tgt'=32] {'tgt'}, use_global_device_ids=true, to_apply=%region_30.31 | all-reduce | flops 4096 | bytes 32768 | tf_op jit(solution)/shard_map/pmax | solution.py:35
  838.0 123.8 %psum.53 = f32[4096]{0:T(1024)S(1)} all-reduce(f32[4096]{0:T(1024)S(1)} %exponential_multiply_fusion), channel_id=1, replica_groups=mesh['src'=8,'tgt'=32] {'tgt'}, use_global_device_ids=true, to_apply=%region_31.32 | all-reduce | flops 4096 | bytes 32768 | tf_op jit(solution)/shard_map/psum | solution.py:36
  961.8 29.4 %while.122 = (s32[]{:T(128)}, f32[1024]{0:T(1024)S(1)}, f32[1024]{0:T(1024)S(1)}, pred[4,2]{1,0:T(4,128)(4,1)S(1)}, f32[4096]{0:T(1024)S(1)}, /*index=5*/f32[409...) while((s32[]{:T(128)}, f32[1024]{0:T(1024)S(1)}, ...), condition=%wide.region_35.36_spmd, body=%wide.region_32.35_spmd.sunk | while | flops 72354840 | bytes 4452827 | solution.py:138
  972.9 1.7 fusion.73
  987.7 1.7 fusion.73
  991.2 16.1 %pmax.47 = f32[1024]{0:T(1024)S(1)} all-reduce(f32[1024]{0:T(1024)S(1)} %get-tuple-element.1712), channel_id=1, replica_groups=mesh['src'=8,'tgt'=32] {'src'}, use_global_device_ids=true, to_apply=%region_36.37 | all-reduce | flops 1024 | bytes 8192 | tf_op jit(solution)/shard_map/pmax | solution.py:42
  1007.4 14.2 %psum.54 = f32[1024]{0:T(1024)S(1)} all-reduce(f32[1024]{0:T(1024)S(1)} %exponential_multiply_fusion.3), channel_id=1, replica_groups=mesh['src'=8,'tgt'=32] {'src'}, use_global_device_ids=true, to_apply=%region_37.38 | all-reduce | flops 1024 | bytes 8192 | tf_op jit(solution)/shard_map/psum | solution.py:43
  1022.2 28.2 %while.123 = (s32[]{:T(128)}, f32[64,1024]{1,0:T(8,128)S(1)}, pred[4,2]{1,0:T(4,128)(4,1)S(1)}, bf16[64,4096]{1,0:T(8,128)(2,1)}, f32[4096]{0:T(1024)S(1)}, /*in...) while((s32[]{:T(128)}, f32[64,1024]{1,0:T(8,128)S(1)}, ...), condition=%wide.region_39.40_spmd, body=%wide.region_38.39_spmd.sunk | while | flops 139001888 | bytes 642002 | solution.py:165
  1022.9 2.7 fusion.77
  1026.5 2.7 fusion.77
  1030.0 2.7 fusion.77
  1033.5 2.7 fusion.77
  1037.0 2.7 fusion.77
  1040.6 2.7 fusion.77
  1044.1 2.7 fusion.77
  1047.6 2.7 fusion.77
  1051.1 71.7 %all-reduce.2.cloned.1.call-done = f32[64,1024]{1,0:T(8,128)} async-done(((f32[64,1024]{1,0:T(8,128)}), f32[64,1024]{1,0:T(8,128)}) %all-reduce.2.cloned.1.call-update) | async-done | bytes 262160 | tf_op jit(solution)/shard_map/psum | solution.py:166
  (460 shorter events, 177.0 us)
Async XLA Ops:
  7.2 1115.6 %all-reduce.2.cloned.1.call-start = ((), (), s32[]{:S(2)}) async-start(), calls=%async_computation | async-start | bytes 524288 | tf_op jit(solution)/shard_map/psum | solution.py:166
  11.1 274.7 %copy-start.2 = (f32[4096]{0:T(1024)S(1)}, f32[4096]{0:T(1024)}, u32[]{:S(2)}) copy-start(f32[4096]{0:T(1024)} %param.23) | copy-start | bytes 49156
  1050.4 0.7 copy-start
  1050.4 73.7 %copy-start.1 = (f32[4096]{0:T(1024)}, f32[4096]{0:T(1024)S(1)}, u32[]{:S(2)}) copy-start(f32[4096]{0:T(1024)S(1)} %get-tuple-element.2825) | copy-start | bytes 49156
Sparse Core Ops, SparseCore 0:
  1051.2 71.4 all-reduce.1
where the time goes:
time: 1130 us
  blocking collectives  837 us (74%)
  matrix products  105 us (9%)
  waiting for transfers between devices  71.7 us (6%)
  other arithmetic  55.1 us (5%)
  local copies, waits for them, and re-layouts  46.1 us (4%)
  between operations  14.2 us (1%)
    psum x3, blocking collectives, row_reduce(): summed = lax.psum(summed * jnp.exp(largest - whole_max), 'tgt')  371 us
    pmax x3, blocking collectives, row_reduce(): whole_max = lax.pmax(largest, 'tgt')  371 us
    dot_general x48, matrix products, tile_distance(): lax.dot_general(source_block, target_block, (((0,), (0,)), ((), ())), pre...  81.5 us
    psum x1, waiting for transfers between devices, per_device(): summed_all = lax.psum(numerator, 'src')  71.7 us
    pmax x3, blocking collectives, col_reduce(): whole_max = lax.pmax(largest, 'src')  52.3 us
    psum x3, blocking collectives, col_reduce(): summed = lax.psum(summed * jnp.exp(largest - whole_max), 'src')  42.5 us
  transfers between devices with their start and end apart: 1, of which 1 were waited for; matrix products, arithmetic and copies ran while one was open for 0% of the time, Pallas kernels for 0%

commit v1 on v0

v1 whole, which is shorter than its diff:
```python
import functools
import math

import jax
import jax.numpy as jnp
from jax import lax
from jax.experimental import pallas as pl
from jax.experimental.pallas import tpu as pltpu
from jax.sharding import PartitionSpec as P

SB = 1024
TB = 512
ITERS = 3
ENTROPIC = 0.05
MARGINAL = 1.0
DAMPING = MARGINAL / (MARGINAL + ENTROPIC)
KAPPA = math.log2(math.e) / ENTROPIC
FORBID = -(2.0**100)
MESH = pl.DeviceIdType.MESH
WIDE = 256
LANES = 128
F32 = jnp.float32
BF16 = jnp.bfloat16


def split3(value):
    high = value.astype(BF16).astype(F32)
    rest = value - high
    middle = rest.astype(BF16).astype(F32)
    return high, middle, rest - middle


def tail_rows(at, parts, ones_at):
    shape = (16, parts[0].shape[1])
    row = lax.broadcasted_iota(jnp.int32, shape, 0)
    tail = jnp.where((row >= ones_at) & (row < ones_at + 3), 1.0, 0.0)
    for offset, part in enumerate(parts):
        tail = jnp.where(row == at + offset, jnp.broadcast_to(part, shape), tail)
    return tail


def lse2(scores):
    largest = jnp.max(scores, axis=0, keepdims=True)
    summed = jnp.sum(jnp.exp2(scores - largest), axis=0, keepdims=True)
    return largest + jnp.log2(summed)


def kernel(
    xs, ys, a_mass, b_mass, s_region, t_region, allowed,
    f_out, g_out, projected,
    x_aug, y_aug, x_t, y_t, partial_row, partial_col, partial_mass,
    row_in, potential, col_in, mass_in,
    row_send, row_recv, pot_send, pot_recv, col_send, col_recv, mass_send, mass_recv,
    *, n_src, n_tgt, comm,
):
    width, n_i = xs.shape
    n_j = ys.shape[1]
    my_src = lax.axis_index("src")
    my_tgt = lax.axis_index("tgt")
    piece = n_i // n_tgt
    share = width // n_src
    src_peer = lambda r: (lax.rem(my_src + r, n_src), my_tgt)
    tgt_peer = lambda r: (my_src, lax.rem(my_tgt + r, n_tgt))

    if comm:
        barrier = pltpu.get_barrier_semaphore()

        @pl.loop(1, n_tgt)
        def _(r):
            pl.semaphore_signal(barrier, inc=1, device_id=tgt_peer(r), device_id_type=MESH)

        @pl.loop(1, n_src)
        def _(r):
            pl.semaphore_signal(barrier, inc=1, device_id=src_peer(r), device_id_type=MESH)

    x = xs[...]
    x_wide = x.astype(F32)
    y_wide = ys[...].astype(F32)
    x_term = jnp.sum(x_wide * x_wide, axis=0, keepdims=True) * (-KAPPA / width)
    y_term = jnp.sum(y_wide * y_wide, axis=0, keepdims=True) * (-KAPPA / width)
    a_log = jnp.log2(a_mass[...])
    b_log = jnp.log2(b_mass[...])
    y_parts = split3(y_wide * (2.0 * KAPPA / width))

    x_aug[0:64, :] = x
    x_aug[64:128, :] = x
    x_aug[192:256, :] = x
    row16 = lax.broadcasted_iota(jnp.int32, (16, n_i), 0)
    col16 = lax.broadcasted_iota(jnp.int32, (16, n_i), 1)
    x_aug[128:144, :] = jnp.where((row16 >= 8) & (row16 < 11), 1.0, 0.0).astype(BF16)
    x_aug[144:160, :] = jnp.where(row16 == col16 // SB, 1.0, 0.0).astype(BF16)
    x_aug[160:192, :] = jnp.zeros((32, n_i), BF16)

    y_aug[0:64, :] = y_parts[0].astype(BF16)
    y_aug[64:128, :] = y_parts[1].astype(BF16)
    y_aug[192:256, :] = y_parts[2].astype(BF16)
    row16 = lax.broadcasted_iota(jnp.int32, (16, n_j), 0)
    col16 = lax.broadcasted_iota(jnp.int32, (16, n_j), 1)
    y_aug[128:144, :] = jnp.where(row16 < 3, 1.0, 0.0).astype(BF16)
    penalty = jnp.zeros((16, n_j), F32)
    for s in range(n_i // SB):
        for t in range(n_j // TB):
            keep = allowed[s_region[s], t_region[t]]
            here = (row16 == s) & (col16 // TB == t)
            penalty = jnp.where(here, jnp.where(keep > 0, 0.0, FORBID), penalty)
    y_aug[144:160, :] = penalty.astype(BF16)
    y_aug[160:192, :] = jnp.zeros((32, n_j), BF16)

    for c in range(n_i // WIDE):
        x_t[c * WIDE : (c + 1) * WIDE, :] = x_aug[:, c * WIDE : (c + 1) * WIDE].T
    for c in range(n_j // WIDE):
        y_t[c * WIDE : (c + 1) * WIDE, :] = y_aug[:, c * WIDE : (c + 1) * WIDE].T

    if comm:
        pl.semaphore_wait(barrier, n_tgt + n_src - 2)

    b_term = b_log + y_term
    col_lse = None
    for it in range(ITERS):
        score_b = b_term if it == 0 else b_term - DAMPING * (col_lse + y_term)
        y_t[:, 128:144] = tail_rows(8, split3(score_b), 0).T.astype(BF16)

        @pl.loop(0, n_i // WIDE)
        def _(c):
            at = pl.ds(pl.multiple_of(c * WIDE, WIDE), WIDE)
            partial_row[it, :, at] = lse2(jnp.dot(y_t[...], x_aug[:, at], preferred_element_type=F32))

        if comm:

            @pl.loop(1, n_tgt)
            def _(r):
                owner = lax.rem(my_tgt + r, n_tgt)
                pltpu.make_async_remote_copy(
                    src_ref=partial_row.at[it, :, pl.ds(pl.multiple_of(owner * piece, piece), piece)],
                    dst_ref=row_in.at[it, r - 1],
                    send_sem=row_send.at[it],
                    recv_sem=row_recv.at[it],
                    device_id=(my_src, owner),
                    device_id_type=MESH,
                ).start()

        mine = pl.ds(pl.multiple_of(my_tgt * piece, piece), piece)
        own = partial_row[it, :, mine]
        if comm:
            pltpu.make_async_copy(row_in.at[it], row_in.at[it], row_recv.at[it]).wait()
            others = row_in[it]
            largest = jnp.maximum(jnp.max(others, axis=0), own)
            summed = jnp.sum(jnp.exp2(others - largest[None]), axis=0) + jnp.exp2(own - largest)
            own = largest + jnp.log2(summed)
        potential[it, :, mine] = own
        if comm:

            @pl.loop(1, n_tgt)
            def _(r):
                pltpu.make_async_remote_copy(
                    src_ref=potential.at[it, :, mine],
                    dst_ref=potential.at[it, :, mine],
                    send_sem=pot_send.at[it],
                    recv_sem=pot_recv.at[it],
                    device_id=tgt_peer(r),
                    device_id_type=MESH,
                ).start()

            rest = potential.at[it, :, pl.ds(0, n_i - piece)]
            pltpu.make_async_copy(rest, rest, pot_recv.at[it]).wait()

        f2 = -DAMPING * (potential[it] + x_term)
        if it == ITERS - 1:
            f_out[...] = f2 * (1.0 / KAPPA)
        score_a = a_log + f2 + x_term
        x_t[:, 128:144] = tail_rows(0, split3(score_a), 8).T.astype(BF16)

        @pl.loop(0, n_j // WIDE)
        def _(c):
            at = pl.ds(pl.multiple_of(c * WIDE, WIDE), WIDE)
            rhs = y_aug[:, at]
            parts = [
                lse2(jnp.dot(x_t[s * SB : (s + 1) * SB, :], rhs, preferred_element_type=F32))
                for s in range(n_i // SB)
            ]
            largest = functools.reduce(jnp.maximum, parts)
            summed = sum(jnp.exp2(part - largest) for part in parts)
            partial_col[it, :, at] = largest + jnp.log2(summed)

        col_lse = partial_col[it]
        if comm:

            @pl.loop(1, n_src)
            def _(r):
                pltpu.make_async_remote_copy(
                    src_ref=partial_col.at[it],
                    dst_ref=col_in.at[it, r - 1],
                    send_sem=col_send.at[it],
                    recv_sem=col_recv.at[it],
                    device_id=src_peer(r),
                    device_id_type=MESH,
                ).start()

            pltpu.make_async_copy(col_in.at[it], col_in.at[it], col_recv.at[it]).wait()
            others = col_in[it]
            largest = jnp.maximum(jnp.max(others, axis=0), col_lse)
            summed = jnp.sum(jnp.exp2(others - largest[None]), axis=0) + jnp.exp2(col_lse - largest)
            col_lse = largest + jnp.log2(summed)

    g_out[...] = (-DAMPING / KAPPA) * (col_lse + y_term)

    y_aug[128:144, :] = tail_rows(8, split3(-col_lse), 0).astype(BF16)

    @pl.loop(0, n_j // WIDE)
    def _(c):
        at = pl.ds(pl.multiple_of(c * WIDE, WIDE), WIDE)
        rhs = y_aug[:, at]
        total = jnp.zeros((width, WIDE), F32)
        for s in range(n_i // SB):
            scores = jnp.dot(x_t[s * SB : (s + 1) * SB, :], rhs, preferred_element_type=F32)
            weight = jnp.exp2(scores).astype(BF16)
            total += jnp.dot(xs[:, s * SB : (s + 1) * SB], weight, preferred_element_type=F32)
        for k in range(n_src):
            partial_mass[k, :, at] = total[k * share : (k + 1) * share]

    result = partial_mass[my_src]
    if comm:

        @pl.loop(1, n_src)
        def _(r):
            owner = lax.rem(my_src + r, n_src)
            pltpu.make_async_remote_copy(
                src_ref=partial_mass.at[owner],
                dst_ref=mass_in.at[r - 1],
                send_sem=mass_send,
                recv_sem=mass_recv,
                device_id=(owner, my_tgt),
                device_id_type=MESH,
            ).start()

        pltpu.make_async_copy(mass_in, mass_in, mass_recv).wait()
        result = result + jnp.sum(mass_in[...], axis=0)
    projected[...] = result

    if comm:
        for it in range(ITERS):
            pltpu.make_async_copy(row_in.at[it], row_in.at[it], row_send.at[it]).wait()
            rest = potential.at[it, :, pl.ds(0, n_i - piece)]
            pltpu.make_async_copy(rest, rest, pot_send.at[it]).wait()
            pltpu.make_async_copy(col_in.at[it], col_in.at[it], col_send.at[it]).wait()
        pltpu.make_async_copy(mass_in, mass_in, mass_send).wait()


def solution(mesh, comm=True):
    n_src, n_tgt = mesh.shape["src"], mesh.shape["tgt"]

    def per_device(xs, ys, a_mass, b_mass, s_region, t_region, allowed):
        width, n_i = xs.shape
        n_j = ys.shape[1]
        share = width // n_src
        piece = n_i // n_tgt
        vmem = pl.BlockSpec(memory_space=pltpu.VMEM)
        smem = pl.BlockSpec(memory_space=pltpu.SMEM)
        dma = pltpu.SemaphoreType.DMA
        f, g, projected = pl.pallas_call(
            functools.partial(kernel, n_src=n_src, n_tgt=n_tgt, comm=comm),
            out_shape=(
                jax.ShapeDtypeStruct((1, n_i), F32),
                jax.ShapeDtypeStruct((1, n_j), F32),
                jax.ShapeDtypeStruct((share, n_j), F32),
            ),
            in_specs=[vmem] * 4 + [smem] * 3,
            out_specs=(vmem, vmem, vmem),
            scratch_shapes=[
                pltpu.VMEM((256, n_i), BF16),
                pltpu.VMEM((256, n_j), BF16),
                pltpu.VMEM((n_i, 256), BF16),
                pltpu.VMEM((n_j, 256), BF16),
                pltpu.VMEM((ITERS, 1, n_i), F32),
                pltpu.VMEM((ITERS, 1, n_j), F32),
                pltpu.VMEM((n_src, share, n_j), F32),
                pltpu.VMEM((ITERS, n_tgt - 1, 1, piece), F32),
                pltpu.VMEM((ITERS, 1, n_i), F32),
                pltpu.VMEM((ITERS, n_src - 1, 1, n_j), F32),
                pltpu.VMEM((n_src - 1, share, n_j), F32),
                dma((ITERS,)), dma((ITERS,)), dma((ITERS,)), dma((ITERS,)),
                dma((ITERS,)), dma((ITERS,)), dma, dma,
            ],
            compiler_params=pltpu.CompilerParams(
                collective_id=0 if comm else None,
                has_side_effects=comm,
                vmem_limit_bytes=48 * 1024 * 1024,
            ),
        )(xs, ys, a_mass.reshape(1, n_i), b_mass.reshape(1, n_j), s_region, t_region, allowed)
        return f.reshape(n_i), g.reshape(n_j), projected

    placed = (P(None, "src"), P(None, "tgt"), P("src"), P("tgt"), P("src"), P("tgt"), P())
    return jax.shard_map(
        per_device,
        mesh=mesh,
        in_specs=placed,
        out_specs=(P("src"), P("tgt"), P("src", "tgt")),
        check_vma=False,
    )
```

time: 1130 us -> 116 us (0.10)
  blocking collectives: 837 us -> 0 us
  Pallas kernels: 0 us -> 108 us
  matrix products: 105 us -> 0 us
  waiting for transfers between devices: 71.7 us -> 0 us
  other arithmetic: 55.1 us -> 0 us
  local copies, waits for them, and re-layouts: 46.1 us -> 6.52 us
  between operations: 14.2 us -> 0.66 us
    pmax x6 -> x0, blocking collectives: 423 us -> none  [the longest x3 371 us: row_reduce(): whole_max = lax.pmax(largest, 'tgt')]
    psum x6 -> x0, blocking collectives: 414 us -> none  [the longest x3 371 us: row_reduce(): summed = lax.psum(summed * jnp.exp(largest - whole_max), 'tgt')]
    pallas_call x0 -> x1, Pallas kernels: none -> 108 us  [per_device(): pl.pallas_call(functools.partial(kernel, n_src=n_src, n_tgt=n_tgt, comm=c...]
    dot_general x57 -> x0, matrix products: 105 us -> none  [the longest x48 81.5 us: tile_distance(): lax.dot_general(source_block, target_block, (((0,), (0,)), ((), ())), pre...]
    psum x1 -> x0, waiting for transfers between devices: 71.7 us -> none  [per_device(): summed_all = lax.psum(numerator, 'src')]
    dynamic_slice x281 -> x0, local copies, waits for them, and re-layouts: 44.6 us -> none  [the longest x24 15.3 us: row_visit(): fresh = tile_pair(compute, tile_allowed[row_block, col_block])]
    dynamic_update_slice x48 -> x0, other arithmetic: 35.5 us -> none  [the longest x24 19.8 us: col_visit(): lax.dynamic_update_slice_in_dim(totals, joined[1], col_block * TB, 0)]
    reduce_sum x50 -> x0, other arithmetic: 18.9 us -> none  [the longest x24 8.64 us: compute(): return (largest, jnp.sum(jnp.exp(scores - largest[None, :]), axis=0))]
  transfers between devices with their start and end apart: 1 -> 0, of which waited for: 1 -> 0; matrix products, arithmetic and copies ran while one was open for 0% -> 0% of each run, Pallas kernels for 0% -> 0%
where the time goes in v1:
time: 116 us; the launch traced here: 115 us
  Pallas kernels  108 us (93%)
  local copies, waits for them, and re-layouts  6.52 us (6%)
    pallas_call x1, Pallas kernels, per_device(): pl.pallas_call(functools.partial(kernel, n_src=n_src, n_tgt=n_tgt, comm=c...  108 us
    unnamed x17, local copies, waits for them, and re-layouts  6.52 us

profile of v1, /device:TPU:2, one launch (start us, length us, event | category | flops | bytes accessed | tf_op | source)
XLA Modules:
  0.0 114.8 jit_solution(1178336899054735691)
XLA Ops:
  0.6 0.0 copy-start.5
  0.6 0.0 copy-start.6
  0.7 0.6 copy-done.5
  1.3 0.0 copy-done.6
  1.3 0.0 copy-start
  1.3 1.0 copy-done
  2.3 0.0 copy-start.1
  2.3 0.9 copy-done.1
  3.3 0.0 copy-start.2
  3.3 0.7 copy-done.2
  4.0 0.0 copy-start.3
  4.0 0.7 copy-done.3
  4.7 0.0 copy-start.4
  4.7 0.7 copy-done.4
  5.4 107.6 %shard_map.94 = (f32[1,4096]{1,0:T(1,128)S(1)}, f32[1,1024]{1,0:T(1,128)S(1)}, f32[8,1024]{1,0:T(8,128)S(1)}) custom-call(bf16[64,4096]{1,0:T(8,128)(2,1)S(1)} %copy-done, bf16[64,1024]{1,0:T(8,128)(2,1)S(1)} %copy-done.1, f32[1,4096]{1,0:T(1,128)S(1)} %bitcast.4, f32[1,1024]{1,0:T(1,128)S(1)} %bitcast.6, s32[4]{0:T(128)S(1)} %copy-done.5, s32[2]{0:T(128)S(1)} %copy-done.6, ...), custom_call_target="tpu_custom_call" | custom-call | tf_op jit(solution)/shard_map/pallas_call | solution.py:260
  113.0 0.6 copy.13
  113.6 0.6 copy.14
  114.2 0.6 copy.15
Async XLA Ops:
  0.6 0.7 copy-start.5
  0.6 0.7 copy-start.6
  1.3 1.0 copy-start
  2.3 0.9 copy-start.1
  3.3 0.7 copy-start.2
  4.0 0.7 copy-start.3
  4.7 0.7 copy-start.4

commit v2 on v1

v2 whole, which is shorter than its diff:
```python
import functools
import math

import jax
import jax.numpy as jnp
from jax import lax
from jax.experimental import pallas as pl
from jax.experimental.pallas import tpu as pltpu
from jax.sharding import PartitionSpec as P

SB = 1024
TB = 512
ITERS = 3
ENTROPIC = 0.05
MARGINAL = 1.0
DAMPING = MARGINAL / (MARGINAL + ENTROPIC)
KAPPA = math.log2(math.e) / ENTROPIC
FORBID = -(2.0**100)
MESH = pl.DeviceIdType.MESH
WIDE = 256
SUB = 256
LANES = 128
TILE = 1024
TAIL = 128
F32 = jnp.float32
BF16 = jnp.bfloat16


def split3(value):
    high = value.astype(BF16).astype(F32)
    rest = value - high
    middle = rest.astype(BF16).astype(F32)
    return [high, middle, rest - middle]


def dot(a, b):
    return jnp.dot(a, b, preferred_element_type=F32)


def join(parts):
    largest = functools.reduce(jnp.maximum, parts)
    return largest + jnp.log2(sum(jnp.exp2(part - largest) for part in parts))


def lse2(scores):
    largest = jnp.max(scores, axis=0, keepdims=True)
    summed = jnp.sum(jnp.exp2(scores - largest), axis=0, keepdims=True)
    return largest, summed


def block_lse(lhs, rows, rhs):
    pairs = [lse2(dot(lhs[at : at + SUB, :], rhs)) for at in range(rows, rows + TILE, SUB)]
    largest = functools.reduce(jnp.maximum, [m for m, _ in pairs])
    summed = sum(l * jnp.exp2(m - largest) for m, l in pairs)
    return largest + jnp.log2(summed)


def gathered_lse(values):
    largest = jnp.max(values, axis=0)
    return largest + jnp.log2(jnp.sum(jnp.exp2(values - largest[None]), axis=0))


def put_potential(dense, into, first):
    stack = jnp.concatenate(split3(dense) + [jnp.zeros((8, LANES), F32)], axis=0)
    columns = stack.T
    lane = lax.broadcasted_iota(jnp.int32, columns.shape, 1)
    for block in range(8):
        own = jnp.where(lane % 8 == block, columns, 0.0)
        rows = slice(first + block * LANES, first + (block + 1) * LANES)
        into[rows, TAIL : TAIL + 24] = own[:, :24].astype(BF16)


def kernel(
    xs_hbm, ys_hbm, a_hbm, b_hbm, s_region, t_region, allowed,
    f_out, g_out, projected,
    xs, ys, a_mass, b_mass, x_aug, y_aug, x_t, y_t, x_term, y_term,
    row_in, col_parts, col_in, numer, lse_in, mass_in,
    load_sem, row_send, row_recv, col_send, col_recv, lse_send, lse_recv, mass_send, mass_recv,
    *, n_src, n_tgt, comm,
):
    width, n_i = xs.shape
    n_j = ys.shape[1]
    tiles = n_i // TILE
    chunks = n_j // WIDE
    per_tile = TILE // WIDE
    share = width // n_src
    my_src = lax.axis_index("src")
    my_tgt = lax.axis_index("tgt")

    loads = [
        pltpu.make_async_copy(source, target, load_sem.at[k])
        for k, (source, target) in enumerate(((xs_hbm, xs), (ys_hbm, ys), (a_hbm, a_mass), (b_hbm, b_mass)))
    ]
    for load in loads:
        load.start()

    if comm:
        barrier = pltpu.get_barrier_semaphore()

        @pl.loop(1, n_tgt)
        def _(r):
            peer = (my_src, lax.rem(my_tgt + r, n_tgt))
            pl.semaphore_signal(barrier, inc=1, device_id=peer, device_id_type=MESH)

        @pl.loop(1, n_src)
        def _(r):
            peer = (lax.rem(my_src + r, n_src), my_tgt)
            pl.semaphore_signal(barrier, inc=1, device_id=peer, device_id_type=MESH)

    def send(src, dst, sent, received, peer):
        pltpu.make_async_remote_copy(
            src_ref=src, dst_ref=dst, send_sem=sent, recv_sem=received, device_id=peer, device_id_type=MESH
        ).start()

    def wait(ref, sem):
        pltpu.make_async_copy(ref, ref, sem).wait()

    for load in loads:
        load.wait()

    x = xs[...]
    x_aug[0:64, :] = x
    x_aug[64:128, :] = x
    x_aug[192:256, :] = x
    row = lax.broadcasted_iota(jnp.int32, (64, n_i), 0)
    col = lax.broadcasted_iota(jnp.int32, (64, n_i), 1)
    x_aug[TAIL : TAIL + 64, :] = jnp.where((row < 24) | (row - 24 == col // SB), 1.0, 0.0).astype(BF16)
    y_wide = ys[...].astype(F32)
    y_parts = split3(y_wide * (2.0 * KAPPA / width))
    y_aug[0:64, :] = y_parts[0].astype(BF16)
    y_aug[64:128, :] = y_parts[1].astype(BF16)
    y_aug[192:256, :] = y_parts[2].astype(BF16)
    row = lax.broadcasted_iota(jnp.int32, (64, n_j), 0)
    col = lax.broadcasted_iota(jnp.int32, (64, n_j), 1)
    tail = jnp.where(row < 24, 1.0, 0.0)
    for s in range(n_i // SB):
        for t in range(n_j // TB):
            keep = allowed[s_region[s], t_region[t]]
            here = (row == 24 + s) & (col // TB == t)
            tail = jnp.where(here, jnp.where(keep > 0, 0.0, FORBID), tail)
    y_aug[TAIL : TAIL + 64, :] = tail.astype(BF16)
    for c in range(n_j // WIDE):
        y_t[c * WIDE : (c + 1) * WIDE, :] = y_aug[:, c * WIDE : (c + 1) * WIDE].T
    y_squares = jnp.sum(y_wide * y_wide, axis=0, keepdims=True) * (-KAPPA / width)
    for c in range(n_j // LANES):
        y_term[c : c + 1, :] = y_squares[:, c * LANES : (c + 1) * LANES]
    x_wide = x.astype(F32)
    x_squares = jnp.sum(x_wide * x_wide, axis=0, keepdims=True) * (-KAPPA / width)
    for c in range(n_i // LANES):
        x_term[c : c + 1, :] = x_squares[:, c * LANES : (c + 1) * LANES]
    put_potential(jnp.log2(b_mass[...]) + y_term[...], y_t, 0)

    def row_sends(it, s, which):
        if comm:
            for r in which:
                mine = row_in.at[it, s, my_tgt]
                peer = (my_src, lax.rem(my_tgt + r, n_tgt))
                send(mine, mine, row_send.at[it, s], row_recv.at[it, s], peer)

    def row_pass(it):
        per = -(-(n_tgt - 1) // per_tile)
        for s in range(tiles):
            for c in range(per_tile):
                at = s * TILE + c * WIDE
                value = block_lse(y_t, 0, x_aug[:, at : at + WIDE])
                for h in range(WIDE // LANES):
                    lane = slice(h * LANES, (h + 1) * LANES)
                    row_in[it, s, my_tgt, c * (WIDE // LANES) + h : c * (WIDE // LANES) + h + 1, :] = value[:, lane]
                if s > 0:
                    row_sends(it, s - 1, range(1 + c * per, min(n_tgt, 1 + (c + 1) * per)))
        row_sends(it, tiles - 1, range(1, n_tgt))

    def source_score(it, s):
        if comm:
            wait(row_in.at[it, s, pl.ds(0, n_tgt - 1)], row_recv.at[it, s])
        term = x_term[s * 8 : (s + 1) * 8, :]
        f2 = -DAMPING * (gathered_lse(row_in[it, s]) + term)
        put_potential(jnp.log2(a_mass[s * 8 : (s + 1) * 8, :]) + f2 + term, x_t, s * TILE)
        return f2

    def iteration(it):
        row_pass(it)

        @pl.when(it == 0)
        def _():
            for c in range(n_i // WIDE):
                x_t[c * WIDE : (c + 1) * WIDE, :] = x_aug[:, c * WIDE : (c + 1) * WIDE].T
            if comm:
                pass

        for s in range(tiles):
            source_score(it, s)
            for c in range(chunks):
                value = block_lse(x_t, s * TILE, y_aug[:, c * WIDE : (c + 1) * WIDE])
                for h in range(WIDE // LANES):
                    lane = slice(h * LANES, (h + 1) * LANES)
                    col_parts[s, c * (WIDE // LANES) + h : c * (WIDE // LANES) + h + 1, :] = value[:, lane]
        col_in[it, my_src] = join([col_parts[s] for s in range(tiles)])
        if comm:
            mine = col_in.at[it, my_src]
            for r in range(1, n_src):
                send(mine, mine, col_send.at[it], col_recv.at[it], (lax.rem(my_src + r, n_src), my_tgt))
            wait(col_in.at[it, pl.ds(0, n_src - 1)], col_recv.at[it])
        term = y_term[...]
        g2 = -DAMPING * (gathered_lse(col_in[it]) + term)
        put_potential(jnp.log2(b_mass[...]) + term + g2, y_t, 0)

    if comm:
        pl.semaphore_wait(barrier, n_tgt + n_src - 2)
    pl.loop(0, ITERS - 1)(iteration)

    last = ITERS - 1
    row_pass(last)
    largest = [None] * chunks
    summed = [None] * chunks
    for s in range(tiles):
        f_out[s * 8 : (s + 1) * 8, :] = source_score(last, s) * (1.0 / KAPPA)
        for c in range(chunks):
            at = slice(c * WIDE, (c + 1) * WIDE)
            scores = dot(x_t[s * TILE : (s + 1) * TILE, :], y_aug[:, at])
            peak = jnp.max(scores, axis=0, keepdims=True)
            if s > 0:
                peak = jnp.maximum(peak, largest[c])
                fade = jnp.exp2(largest[c] - peak)
            weight = jnp.exp2(scores - peak)
            total = jnp.sum(weight, axis=0, keepdims=True)
            product = dot(xs[:, s * TILE : (s + 1) * TILE], weight.astype(BF16))
            if s > 0:
                total += summed[c] * fade
                product += numer[:, at] * fade
            largest[c], summed[c] = peak, total
            if s < tiles - 1:
                numer[:, at] = product
                continue
            numer[:, at] = product / total
            value = peak + jnp.log2(total)
            for h in range(WIDE // LANES):
                lane = slice(h * LANES, (h + 1) * LANES)
                lse_in[my_src, c * (WIDE // LANES) + h : c * (WIDE // LANES) + h + 1, :] = value[:, lane]
            mass_in[my_src, :, at] = numer[pl.ds(pl.multiple_of(my_src * share, share), share), at]
            if comm:
                for r in range(1, n_src):
                    owner = lax.rem(my_src + r, n_src)
                    send(
                        numer.at[pl.ds(pl.multiple_of(owner * share, share), share), at],
                        mass_in.at[my_src, :, at],
                        mass_send, mass_recv, (owner, my_tgt),
                    )
    if comm:
        mine = lse_in.at[my_src]
        for r in range(1, n_src):
            send(mine, mine, lse_send, lse_recv, (lax.rem(my_src + r, n_src), my_tgt))
        wait(lse_in.at[pl.ds(0, n_src - 1)], lse_recv)
    col_lse = gathered_lse(lse_in[...])
    g_out[...] = (-DAMPING / KAPPA) * (col_lse + y_term[...])
    scale = jnp.exp2(lse_in[...] - col_lse[None])
    if comm:
        wait(mass_in.at[pl.ds(0, n_src - 1)], mass_recv)
    for c in range(n_j // LANES):
        at = slice(c * LANES, (c + 1) * LANES)
        projected[:, at] = sum(mass_in[d, :, at] * scale[d, c : c + 1, :] for d in range(n_src))

    if comm:
        for it in range(ITERS):
            for s in range(tiles):
                wait(row_in.at[it, s, pl.ds(0, n_tgt - 1)], row_send.at[it, s])
            if it < last:
                wait(col_in.at[it, pl.ds(0, n_src - 1)], col_send.at[it])
        wait(lse_in.at[pl.ds(0, n_src - 1)], lse_send)
        wait(mass_in.at[pl.ds(0, n_src - 1)], mass_send)


def solution(mesh):
    return local(mesh, mesh.shape["src"], mesh.shape["tgt"])


def local(mesh, n_src, n_tgt, comm=True):
    def per_device(xs, ys, a_mass, b_mass, s_region, t_region, allowed):
        width, n_i = xs.shape
        n_j = ys.shape[1]
        share = width // n_src
        tiles = n_i // TILE
        vmem = pl.BlockSpec(memory_space=pltpu.VMEM)
        smem = pl.BlockSpec(memory_space=pltpu.SMEM)
        hbm = pl.BlockSpec(memory_space=pltpu.HBM)
        dma = pltpu.SemaphoreType.DMA
        f, g, projected = pl.pallas_call(
            functools.partial(kernel, n_src=n_src, n_tgt=n_tgt, comm=comm),
            out_shape=(
                jax.ShapeDtypeStruct((n_i // LANES, LANES), F32),
                jax.ShapeDtypeStruct((n_j // LANES, LANES), F32),
                jax.ShapeDtypeStruct((share, n_j), F32),
            ),
            in_specs=[hbm] * 4 + [smem] * 3,
            out_specs=(vmem, vmem, vmem),
            scratch_shapes=[
                pltpu.VMEM((width, n_i), BF16),
                pltpu.VMEM((width, n_j), BF16),
                pltpu.VMEM((n_i // LANES, LANES), F32),
                pltpu.VMEM((n_j // LANES, LANES), F32),
                pltpu.VMEM((256, n_i), BF16),
                pltpu.VMEM((256, n_j), BF16),
                pltpu.VMEM((n_i, 256), BF16),
                pltpu.VMEM((n_j, 256), BF16),
                pltpu.VMEM((n_i // LANES, LANES), F32),
                pltpu.VMEM((n_j // LANES, LANES), F32),
                pltpu.VMEM((ITERS, tiles, n_tgt, 8, LANES), F32),
                pltpu.VMEM((tiles, 8, LANES), F32),
                pltpu.VMEM((ITERS, n_src, 8, LANES), F32),
                pltpu.VMEM((width, n_j), F32),
                pltpu.VMEM((n_src, 8, LANES), F32),
                pltpu.VMEM((n_src, share, n_j), F32),
                dma((4,)),
                dma((ITERS, tiles)), dma((ITERS, tiles)), dma((ITERS,)), dma((ITERS,)),
                dma, dma, dma, dma,
            ],
            compiler_params=pltpu.CompilerParams(
                collective_id=0 if comm else None,
                has_side_effects=comm,
                vmem_limit_bytes=48 * 1024 * 1024,
            ),
        )(
            xs, ys, a_mass.reshape(n_i // LANES, LANES), b_mass.reshape(n_j // LANES, LANES),
            s_region, t_region, allowed,
        )
        return f.reshape(n_i), g.reshape(n_j), projected

    placed = (P(None, "src"), P(None, "tgt"), P("src"), P("tgt"), P("src"), P("tgt"), P())
    return jax.shard_map(
        per_device,
        mesh=mesh,
        in_specs=placed,
        out_specs=(P("src"), P("tgt"), P("src", "tgt")),
        check_vma=False,
    )
```

time: 116 us -> 80.2 us (0.69)
  Pallas kernels: 108 us -> 71.4 us
    pallas_call x1, Pallas kernels: 108 us -> 71.4 us  [per_device(): pl.pallas_call(functools.partial(kernel, n_src=n_src, n_tgt=n_tgt, comm=c...]
where the time goes in v2:
time: 80.2 us; the launch traced here: 78.6 us
  Pallas kernels  71.4 us (89%)
  local copies, waits for them, and re-layouts  6.52 us (8%)
    pallas_call x1, Pallas kernels, per_device(): pl.pallas_call(functools.partial(kernel, n_src=n_src, n_tgt=n_tgt, comm=c...  71.4 us
    unnamed x17, local copies, waits for them, and re-layouts  6.52 us

profile of v2, /device:TPU:2, one launch (start us, length us, event | category | flops | bytes accessed | tf_op | source)
XLA Modules:
  0.0 78.6 jit_solution(15351395710868402336)
XLA Ops:
  0.6 0.0 copy-start.5
  0.6 0.0 copy-start.6
  0.7 0.6 copy-done.5
  1.3 0.0 copy-done.6
  1.3 0.0 copy-start
  1.3 1.0 %copy-done = bf16[64,4096]{1,0:T(8,128)(2,1)S(1)} copy-done((bf16[64,4096]{1,0:T(8,128)(2,1)S(1)}, bf16[64,4096]{1,0:T(8,128)(2,1)}, u32[]{:S(2)}) %copy-start) | copy-done | bytes 524312
  2.3 0.0 copy-start.1
  2.3 0.9 %copy-done.1 = bf16[64,1024]{1,0:T(8,128)(2,1)S(1)} copy-done((bf16[64,1024]{1,0:T(8,128)(2,1)S(1)}, bf16[64,1024]{1,0:T(8,128)(2,1)}, u32[]{:S(2)}) %copy-start.1) | copy-done | bytes 131096
  3.3 0.0 copy-start.2
  3.3 0.7 copy-done.2
  4.0 0.0 copy-start.3
  4.0 0.7 copy-done.3
  4.7 0.0 copy-start.4
  4.7 0.7 copy-done.4
  5.4 71.4 %shard_map.94 = (f32[32,128]{1,0:T(8,128)S(1)}, f32[8,128]{1,0:T(8,128)S(1)}, f32[8,1024]{1,0:T(8,128)S(1)}) custom-call(bf16[64,4096]{1,0:T(8,128)(2,1)S(1)} %copy-done, bf16[64,1024]{1,0:T(8,128)(2,1)S(1)} %copy-done.1, f32[32,128]{1,0:T(8,128)S(1)} %bitcast.4, f32[8,128]{1,0:T(8,128)S(1)} %bitcast.6, s32[4]{0:T(128)S(1)} %copy-done.5, s32[2]{0:T(128)S(1)} %copy-done.6, ...), custom_call_target="tpu_custom_call" | custom-call | tf_op jit(solution)/shard_map/pallas_call | solution.py:287
  76.8 0.6 copy.13
  77.4 0.6 copy.14
  78.0 0.6 copy.15
Async XLA Ops:
  0.6 0.7 copy-start.5
  0.6 0.7 copy-start.6
  1.3 1.0 %copy-start = (bf16[64,4096]{1,0:T(8,128)(2,1)S(1)}, bf16[64,4096]{1,0:T(8,128)(2,1)}, u32[]{:S(2)}) copy-start(bf16[64,4096]{1,0:T(8,128)(2,1)} %xs_hbm.1) | copy-start | bytes 1572868
  2.3 0.9 %copy-start.1 = (bf16[64,1024]{1,0:T(8,128)(2,1)S(1)}, bf16[64,1024]{1,0:T(8,128)(2,1)}, u32[]{:S(2)}) copy-start(bf16[64,1024]{1,0:T(8,128)(2,1)} %ys_hbm.1) | copy-start | bytes 393220
  3.3 0.7 copy-start.2
  4.0 0.7 copy-start.3
  4.7 0.7 copy-start.4

commit v3 on v1

v3 whole, which is shorter than its diff:
```python
import functools
import math

import jax
import jax.numpy as jnp
from jax import lax
from jax.experimental import pallas as pl
from jax.experimental.pallas import tpu as pltpu
from jax.sharding import PartitionSpec as P

SB = 1024
TB = 512
ITERS = 3
ENTROPIC = 0.05
MARGINAL = 1.0
DAMPING = MARGINAL / (MARGINAL + ENTROPIC)
KAPPA = math.log2(math.e) / ENTROPIC
FORBID = -(2.0**100)
MESH = pl.DeviceIdType.MESH
WIDE = 256
SUB = 256
ROWS = 32
LANES = 128
TILE = 1024
TAIL = 128
POT = TAIL + 32
VMEM_MIB = 63
F32 = jnp.float32
BF16 = jnp.bfloat16


def split3(value):
    high = value.astype(BF16).astype(F32)
    rest = value - high
    middle = rest.astype(BF16).astype(F32)
    return [high, middle, rest - middle]


def dot(a, b):
    return jnp.dot(a, b, preferred_element_type=F32)


def block_lse(lhs, rhs):
    peaks, sums = [], []
    for at in range(0, lhs.shape[0], SUB):
        scores = dot(lhs[at : at + SUB, :], rhs).reshape(SUB // 8, 8, rhs.shape[1])
        peak = jnp.max(scores, axis=0)
        peaks.append(peak)
        sums.append(jnp.sum(jnp.exp2(scores - peak[None]), axis=0))
    largest = functools.reduce(jnp.maximum, peaks)
    summed = sum(total * jnp.exp2(peak - largest) for peak, total in zip(peaks, sums))
    peak = jnp.max(largest, axis=0, keepdims=True)
    return peak + jnp.log2(jnp.sum(summed * jnp.exp2(largest - peak), axis=0, keepdims=True))


def joined(values, logs):
    if not logs:
        return jnp.sum(values, axis=0)
    largest = jnp.max(values, axis=0)
    return largest + jnp.log2(jnp.sum(jnp.exp2(values - largest[None]), axis=0))


def or_nan(safe, value):
    return jnp.where(safe, value, jnp.nan)


def put_potential(dense, into):
    stack = jnp.concatenate(split3(dense) + [jnp.zeros((8, LANES), F32)], axis=0)
    columns = stack.T
    lane = lax.broadcasted_iota(jnp.int32, columns.shape, 1)
    for block in range(8):
        own = jnp.where(lane % 8 == block, columns, 0.0)
        into[block * LANES : (block + 1) * LANES, TAIL : TAIL + 24] = own[:, :24].astype(BF16)


def lane_row(dense):
    return jnp.concatenate([dense[r : r + 1, :] for r in range(8)], axis=1)


def fold_lanes(values):
    return sum(values[:, at : at + LANES] for at in range(0, values.shape[1], LANES))


def farthest_first(n_src, n_tgt):
    hops = lambda d, n: min(d, n - d)
    chips = [(r // 4, r % 4) for r in range(1, n_tgt // 2)]
    chips.sort(key=lambda o: -(hops(o[0], n_tgt // 8) + hops(o[1], 4)))
    return sorted(range(1, n_src), key=lambda r: -hops(r, n_src)), chips


def kernel(
    xs_hbm, ys_hbm, a_hbm, b_hbm, s_region, t_region, allowed,
    f_out, g_out, projected,
    ys, a_mass, b_mass, x_aug, y_aug, y_t, x_t, x_term, y_term, coupling, w_col, acc, first_f, last_f,
    pair_in, row_in, col_in, numer, numer_t, mass_in,
    load_sem, pair_send, pair_recv, row_send, row_recv, col_send, col_recv, mass_send, mass_recv,
    *, n_src, n_tgt, comm,
):
    width, n_j = ys.shape
    n_i = x_aug.shape[1]
    tiles = n_i // TILE
    chips = n_tgt // 2
    share = width // n_src
    src_order, chip_order = farthest_first(n_src, n_tgt)
    my_src = lax.axis_index("src")
    my_tgt = lax.axis_index("tgt")
    my_core = my_tgt % 2
    my_chip = my_tgt // 2
    sibling = (my_src, my_tgt + 1 - 2 * my_core)

    def chip_peer(offset):
        y = lax.rem(my_chip // 4 + offset[0], n_tgt // 8)
        return (my_src, (y * 4 + lax.rem(my_chip + offset[1], 4)) * 2 + my_core)

    def src_peer(offset):
        return (lax.rem(my_src + offset, n_src), my_tgt)

    loads = [
        pltpu.make_async_copy(source, target, load_sem.at[k])
        for k, (source, target) in enumerate((
            (ys_hbm, ys), (b_hbm, b_mass), (xs_hbm, x_aug.at[0:64]), (xs_hbm, x_aug.at[64:128]),
            (xs_hbm, x_aug.at[192:256]), (a_hbm, a_mass),
        ))
    ]
    for load in loads:
        load.start()

    if comm:
        barrier = pltpu.get_barrier_semaphore()
        peers = [sibling] + [chip_peer(o) for o in chip_order] + [src_peer(o) for o in src_order]
        for peer in peers:
            pl.semaphore_signal(barrier, inc=1, device_id=peer, device_id_type=MESH)

    def send(src, dst, sent, received, peer):
        pltpu.make_async_remote_copy(
            src_ref=src, dst_ref=dst, send_sem=sent, recv_sem=received, device_id=peer, device_id_type=MESH
        ).start()

    def wait(ref, sem):
        pltpu.make_async_copy(ref, ref, sem).wait()

    row = lax.broadcasted_iota(jnp.int32, (64, n_i), 0)
    col = lax.broadcasted_iota(jnp.int32, (64, n_i), 1)
    x_aug[TAIL : TAIL + 64, :] = jnp.where((row < 24) | (row - 24 == col // SB), 1.0, 0.0).astype(BF16)
    row = lax.broadcasted_iota(jnp.int32, (8, n_j), 0)
    col = lax.broadcasted_iota(jnp.int32, (8, n_j), 1)
    mask = jnp.zeros((8, n_j), F32)
    for s in range(n_i // SB):
        for t in range(n_j // TB):
            keep = allowed[s_region[s], t_region[t]]
            here = (row == s) & (col // TB == t)
            mask = jnp.where(here, jnp.where(keep > 0, 0.0, FORBID), mask)
    ones = jnp.where(row < 3, 1.0, 0.0)
    tail = [jnp.zeros((24, n_j), F32), mask, ones, jnp.zeros((24, n_j), F32)]
    y_aug[TAIL : TAIL + 64, :] = jnp.concatenate(tail, axis=0).astype(BF16)
    for load in loads[:2]:
        load.wait()
    y_wide = ys[...].astype(F32)
    y_parts = split3(y_wide * (2.0 * KAPPA / width))
    y_aug[0:64, :] = y_parts[0].astype(BF16)
    y_aug[64:128, :] = y_parts[1].astype(BF16)
    y_aug[192:256, :] = y_parts[2].astype(BF16)
    for c in range(n_j // WIDE):
        y_t[c * WIDE : (c + 1) * WIDE, :] = y_aug[:, c * WIDE : (c + 1) * WIDE].T
    y_squares = jnp.sum(y_wide * y_wide, axis=0, keepdims=True) * (-KAPPA / width)
    for c in range(n_j // LANES):
        y_term[c : c + 1, :] = y_squares[:, c * LANES : (c + 1) * LANES]
    b_log = jnp.log2(b_mass[...])
    put_potential(b_log + y_term[...], y_t)
    for load in loads[2:]:
        load.wait()

    def pair_send_tile(it, s):
        if comm:
            mine = pair_in.at[it, s, my_core]
            send(mine, mine, pair_send.at[it, s], pair_recv.at[it, s], sibling)

    def chip_send_tile(it, s):
        if comm:
            wait(pair_in.at[it, s, 0], pair_recv.at[it, s])
        row_in[it, s, my_chip] = joined(pair_in[it, s], it == 0)
        if comm:
            mine = row_in.at[it, s, my_chip]
            for offset in chip_order:
                send(mine, mine, row_send.at[it, s], row_recv.at[it, s], chip_peer(offset))

    def row_total(it, s):
        if comm:
            wait(row_in.at[it, s, pl.ds(0, chips - 1)], row_recv.at[it, s])
        return joined(row_in[it, s], it == 0)

    def tile_of(s):
        return slice(s * 8, (s + 1) * 8)

    def source_factor(it, s):
        total = row_total(it, s)
        a_log = jnp.log2(a_mass[tile_of(s), :])
        first = first_f[tile_of(s), :]
        f2 = -DAMPING * (jnp.log2(total) - a_log - first)
        safe = (total >= 2.0**-28) & (jnp.abs(f2 - first) <= 30.0)
        if it > 1:
            safe &= jnp.abs(f2 - last_f[tile_of(s), :]) <= 8.0
        f2 = or_nan(safe, f2)
        last_f[tile_of(s), :] = f2
        return jnp.exp2(f2 - first), f2

    def target_total(it):
        for r in range(8):
            part = jnp.sum(acc[r * LANES : (r + 1) * LANES, :].T, axis=0, keepdims=True)
            col_in[it, my_src, r : r + 1, :] = part
        if comm:
            mine = col_in.at[it, my_src]
            for offset in src_order:
                send(mine, mine, col_send.at[it], col_recv.at[it], src_peer(offset))
            wait(col_in.at[it, pl.ds(0, n_src - 1)], col_recv.at[it])
        return jnp.sum(col_in[it], axis=0)

    def target_factor(it):
        total = target_total(it)
        g2 = -DAMPING * (jnp.log2(total) - b_log)
        w = jnp.exp2(or_nan(total >= 2.0 ** (-60.0 if it == 0 else -50.0), g2))
        for r in range(8):
            w_col[r * LANES : (r + 1) * LANES, :] = jnp.broadcast_to(w[r : r + 1, :], (LANES, LANES)).T

    for s in range(tiles):
        for c in range(TILE // WIDE):
            at = s * TILE + c * WIDE
            value = block_lse(y_t, x_aug[:, at : at + WIDE])
            for h in range(WIDE // LANES):
                r = c * (WIDE // LANES) + h
                pair_in[0, s, my_core, r : r + 1, :] = value[:, h * LANES : (h + 1) * LANES]
        if comm and s == 0:
            pl.semaphore_wait(barrier, len(peers))
        pair_send_tile(0, s)
        if s > 0:
            chip_send_tile(0, s - 1)
    x_wide = x_aug[0:64, :].astype(F32)
    x_squares = jnp.sum(x_wide * x_wide, axis=0, keepdims=True) * (-KAPPA / width)
    for c in range(n_i // LANES):
        x_term[c : c + 1, :] = x_squares[:, c * LANES : (c + 1) * LANES]
    chip_send_tile(0, tiles - 1)
    for c in range(n_i // WIDE):
        x_t[c * WIDE : (c + 1) * WIDE, :] = x_aug[0:128, c * WIDE : (c + 1) * WIDE].T

    row16 = lax.broadcasted_iota(jnp.int32, (16, TILE), 0)
    for s in range(tiles):
        whole = row_total(0, s) + x_term[tile_of(s), :]
        a_log = jnp.log2(a_mass[tile_of(s), :])
        scale = a_log + (1.0 - DAMPING) * whole
        f2 = or_nan(jnp.abs(scale) <= 30.0, -DAMPING * whole)
        first_f[tile_of(s), :] = f2
        last_f[tile_of(s), :] = f2
        score = jnp.zeros((16, TILE), F32)
        for k, part in enumerate(split3(a_log + f2 + x_term[tile_of(s), :])):
            score = jnp.where(row16 == k, lane_row(part), score)
        x_aug[POT : POT + 16, s * TILE : (s + 1) * TILE] = score.astype(BF16)
        for c in range(TILE // WIDE):
            at = slice(s * TILE + c * WIDE, s * TILE + (c + 1) * WIDE)
            rhs = x_aug[:, at]
            for j in range(0, n_j, SUB):
                block = jnp.exp2(dot(y_t[j : j + SUB, :], rhs))
                coupling[j : j + SUB, at] = block
                part = fold_lanes(block)
                acc[j : j + SUB, :] = part if s == 0 and c == 0 else acc[j : j + SUB, :] + part
    target_factor(0)

    def row_sweep(it):
        for s in range(tiles):
            sums = jnp.zeros((8, TILE), F32)
            for j in range(0, n_j, ROWS):
                w = jnp.concatenate([w_col[j : j + ROWS, :]] * (TILE // LANES), axis=1)
                block = coupling[j : j + ROWS, s * TILE : (s + 1) * TILE] * w
                sums += jnp.sum(block.reshape(ROWS // 8, 8, TILE), axis=0)
            value = jnp.sum(sums, axis=0, keepdims=True)
            for r in range(8):
                pair_in[it, s, my_core, r : r + 1, :] = value[:, r * LANES : (r + 1) * LANES]
            pair_send_tile(it, s)
        for s in range(tiles):
            chip_send_tile(it, s)

    for it in range(1, ITERS - 1):
        row_sweep(it)
        for s in range(tiles):
            factor = lane_row(source_factor(it, s)[0])
            for j in range(0, n_j, ROWS):
                block = coupling[j : j + ROWS, s * TILE : (s + 1) * TILE] * factor
                part = fold_lanes(block)
                acc[j : j + ROWS, :] = part if s == 0 else acc[j : j + ROWS, :] + part
        target_factor(it)

    last = ITERS - 1
    row_sweep(last)
    for s in range(tiles):
        factor, f2 = source_factor(last, s)
        f_out[tile_of(s), :] = f2 * (1.0 / KAPPA)
        factor = lane_row(factor)
        for j in range(0, n_j, SUB):
            rows = slice(j, j + SUB)
            weight = coupling[rows, s * TILE : (s + 1) * TILE] * factor
            part = fold_lanes(weight)
            product = dot(weight.astype(BF16), x_t[s * TILE : (s + 1) * TILE, :])
            if s > 0:
                part += acc[rows, :]
                product += numer[rows, :]
            acc[rows, :] = part
            numer[rows, :] = product
            if s < tiles - 1:
                continue
            flat = product.T
            for d in range(n_src):
                numer_t[d, :, rows] = flat[d * share : (d + 1) * share, :]
            mass_in[my_src, :, rows] = numer_t[my_src, :, rows]
            if comm:
                for offset in src_order:
                    owner = lax.rem(my_src + offset, n_src)
                    send(
                        numer_t.at[owner, :, rows], mass_in.at[my_src, :, rows],
                        mass_send, mass_recv, (owner, my_tgt),
                    )
    total = target_total(last)
    g_out[...] = (-DAMPING / KAPPA) * (jnp.log2(total) - b_log)
    if comm:
        wait(mass_in.at[pl.ds(0, n_src - 1)], mass_recv)
    projected[...] = jnp.sum(mass_in[...], axis=0) / lane_row(total)

    if comm:
        for it in range(ITERS):
            for s in range(tiles):
                wait(pair_in.at[it, s, 0], pair_send.at[it, s])
                wait(row_in.at[it, s, pl.ds(0, chips - 1)], row_send.at[it, s])
            wait(col_in.at[it, pl.ds(0, n_src - 1)], col_send.at[it])
        wait(mass_in.at[pl.ds(0, n_src - 1)], mass_send)


def tail_rows(at, parts, ones_at):
    shape = (16, parts[0].shape[1])
    row = lax.broadcasted_iota(jnp.int32, shape, 0)
    tail = jnp.where((row >= ones_at) & (row < ones_at + 3), 1.0, 0.0)
    for offset, part in enumerate(parts):
        tail = jnp.where(row == at + offset, jnp.broadcast_to(part, shape), tail)
    return tail


def careful_lse(scores):
    largest = jnp.max(scores, axis=0, keepdims=True)
    summed = jnp.sum(jnp.exp2(scores - largest), axis=0, keepdims=True)
    return largest + jnp.log2(summed)


def careful_kernel(
    xs, ys, a_mass, b_mass, s_region, t_region, allowed,
    f_out, g_out, projected,
    x_aug, y_aug, x_t, y_t, partial_row, partial_col, partial_mass,
    row_in, potential, col_in, mass_in,
    row_send, row_recv, pot_send, pot_recv, col_send, col_recv, mass_send, mass_recv,
    *, n_src, n_tgt,
):
    width, n_i = xs.shape
    n_j = ys.shape[1]
    my_src = lax.axis_index("src")
    my_tgt = lax.axis_index("tgt")
    piece = n_i // n_tgt
    share = width // n_src
    src_peer = lambda r: (lax.rem(my_src + r, n_src), my_tgt)
    tgt_peer = lambda r: (my_src, lax.rem(my_tgt + r, n_tgt))

    barrier = pltpu.get_barrier_semaphore()

    @pl.loop(1, n_tgt)
    def _(r):
        pl.semaphore_signal(barrier, inc=1, device_id=tgt_peer(r), device_id_type=MESH)

    @pl.loop(1, n_src)
    def _(r):
        pl.semaphore_signal(barrier, inc=1, device_id=src_peer(r), device_id_type=MESH)

    x = xs[...]
    x_wide = x.astype(F32)
    y_wide = ys[...].astype(F32)
    x_term = jnp.sum(x_wide * x_wide, axis=0, keepdims=True) * (-KAPPA / width)
    y_term = jnp.sum(y_wide * y_wide, axis=0, keepdims=True) * (-KAPPA / width)
    a_log = jnp.log2(a_mass[...])
    b_log = jnp.log2(b_mass[...])
    y_parts = split3(y_wide * (2.0 * KAPPA / width))

    x_aug[0:64, :] = x
    x_aug[64:128, :] = x
    x_aug[192:256, :] = x
    row16 = lax.broadcasted_iota(jnp.int32, (16, n_i), 0)
    col16 = lax.broadcasted_iota(jnp.int32, (16, n_i), 1)
    x_aug[128:144, :] = jnp.where((row16 >= 8) & (row16 < 11), 1.0, 0.0).astype(BF16)
    x_aug[144:160, :] = jnp.where(row16 == col16 // SB, 1.0, 0.0).astype(BF16)
    x_aug[160:192, :] = jnp.zeros((32, n_i), BF16)

    y_aug[0:64, :] = y_parts[0].astype(BF16)
    y_aug[64:128, :] = y_parts[1].astype(BF16)
    y_aug[192:256, :] = y_parts[2].astype(BF16)
    row16 = lax.broadcasted_iota(jnp.int32, (16, n_j), 0)
    col16 = lax.broadcasted_iota(jnp.int32, (16, n_j), 1)
    y_aug[128:144, :] = jnp.where(row16 < 3, 1.0, 0.0).astype(BF16)
    penalty = jnp.zeros((16, n_j), F32)
    for s in range(n_i // SB):
        for t in range(n_j // TB):
            keep = allowed[s_region[s], t_region[t]]
            here = (row16 == s) & (col16 // TB == t)
            penalty = jnp.where(here, jnp.where(keep > 0, 0.0, FORBID), penalty)
    y_aug[144:160, :] = penalty.astype(BF16)
    y_aug[160:192, :] = jnp.zeros((32, n_j), BF16)

    for c in range(n_i // WIDE):
        x_t[c * WIDE : (c + 1) * WIDE, :] = x_aug[:, c * WIDE : (c + 1) * WIDE].T
    for c in range(n_j // WIDE):
        y_t[c * WIDE : (c + 1) * WIDE, :] = y_aug[:, c * WIDE : (c + 1) * WIDE].T

    pl.semaphore_wait(barrier, n_tgt + n_src - 2)

    b_term = b_log + y_term
    col_lse = None
    for it in range(ITERS):
        score_b = b_term if it == 0 else b_term - DAMPING * (col_lse + y_term)
        y_t[:, 128:144] = tail_rows(8, split3(score_b), 0).T.astype(BF16)

        @pl.loop(0, n_i // WIDE)
        def _(c):
            at = pl.ds(pl.multiple_of(c * WIDE, WIDE), WIDE)
            partial_row[it, :, at] = careful_lse(jnp.dot(y_t[...], x_aug[:, at], preferred_element_type=F32))


        @pl.loop(1, n_tgt)
        def _(r):
            owner = lax.rem(my_tgt + r, n_tgt)
            pltpu.make_async_remote_copy(
                src_ref=partial_row.at[it, :, pl.ds(pl.multiple_of(owner * piece, piece), piece)],
                dst_ref=row_in.at[it, r - 1],
                send_sem=row_send.at[it],
                recv_sem=row_recv.at[it],
                device_id=(my_src, owner),
                device_id_type=MESH,
            ).start()

        mine = pl.ds(pl.multiple_of(my_tgt * piece, piece), piece)
        own = partial_row[it, :, mine]
        pltpu.make_async_copy(row_in.at[it], row_in.at[it], row_recv.at[it]).wait()
        others = row_in[it]
        largest = jnp.maximum(jnp.max(others, axis=0), own)
        summed = jnp.sum(jnp.exp2(others - largest[None]), axis=0) + jnp.exp2(own - largest)
        own = largest + jnp.log2(summed)
        potential[it, :, mine] = own

        @pl.loop(1, n_tgt)
        def _(r):
            pltpu.make_async_remote_copy(
                src_ref=potential.at[it, :, mine],
                dst_ref=potential.at[it, :, mine],
                send_sem=pot_send.at[it],
                recv_sem=pot_recv.at[it],
                device_id=tgt_peer(r),
                device_id_type=MESH,
            ).start()

        rest = potential.at[it, :, pl.ds(0, n_i - piece)]
        pltpu.make_async_copy(rest, rest, pot_recv.at[it]).wait()

        f2 = -DAMPING * (potential[it] + x_term)
        if it == ITERS - 1:
            f_out[...] = f2 * (1.0 / KAPPA)
        score_a = a_log + f2 + x_term
        x_t[:, 128:144] = tail_rows(0, split3(score_a), 8).T.astype(BF16)

        @pl.loop(0, n_j // WIDE)
        def _(c):
            at = pl.ds(pl.multiple_of(c * WIDE, WIDE), WIDE)
            rhs = y_aug[:, at]
            parts = [
                careful_lse(jnp.dot(x_t[s * SB : (s + 1) * SB, :], rhs, preferred_element_type=F32))
                for s in range(n_i // SB)
            ]
            largest = functools.reduce(jnp.maximum, parts)
            summed = sum(jnp.exp2(part - largest) for part in parts)
            partial_col[it, :, at] = largest + jnp.log2(summed)

        col_lse = partial_col[it]

        @pl.loop(1, n_src)
        def _(r):
            pltpu.make_async_remote_copy(
                src_ref=partial_col.at[it],
                dst_ref=col_in.at[it, r - 1],
                send_sem=col_send.at[it],
                recv_sem=col_recv.at[it],
                device_id=src_peer(r),
                device_id_type=MESH,
            ).start()

        pltpu.make_async_copy(col_in.at[it], col_in.at[it], col_recv.at[it]).wait()
        others = col_in[it]
        largest = jnp.maximum(jnp.max(others, axis=0), col_lse)
        summed = jnp.sum(jnp.exp2(others - largest[None]), axis=0) + jnp.exp2(col_lse - largest)
        col_lse = largest + jnp.log2(summed)

    g_out[...] = (-DAMPING / KAPPA) * (col_lse + y_term)

    y_aug[128:144, :] = tail_rows(8, split3(-col_lse), 0).astype(BF16)

    @pl.loop(0, n_j // WIDE)
    def _(c):
        at = pl.ds(pl.multiple_of(c * WIDE, WIDE), WIDE)
        rhs = y_aug[:, at]
        total = jnp.zeros((width, WIDE), F32)
        for s in range(n_i // SB):
            scores = jnp.dot(x_t[s * SB : (s + 1) * SB, :], rhs, preferred_element_type=F32)
            weight = jnp.exp2(scores).astype(BF16)
            total += jnp.dot(xs[:, s * SB : (s + 1) * SB], weight, preferred_element_type=F32)
        for k in range(n_src):
            partial_mass[k, :, at] = total[k * share : (k + 1) * share]

    result = partial_mass[my_src]

    @pl.loop(1, n_src)
    def _(r):
        owner = lax.rem(my_src + r, n_src)
        pltpu.make_async_remote_copy(
            src_ref=partial_mass.at[owner],
            dst_ref=mass_in.at[r - 1],
            send_sem=mass_send,
            recv_sem=mass_recv,
            device_id=(owner, my_tgt),
            device_id_type=MESH,
        ).start()

    pltpu.make_async_copy(mass_in, mass_in, mass_recv).wait()
    result = result + jnp.sum(mass_in[...], axis=0)
    projected[...] = result

    for it in range(ITERS):
        pltpu.make_async_copy(row_in.at[it], row_in.at[it], row_send.at[it]).wait()
        rest = potential.at[it, :, pl.ds(0, n_i - piece)]
        pltpu.make_async_copy(rest, rest, pot_send.at[it]).wait()
        pltpu.make_async_copy(col_in.at[it], col_in.at[it], col_send.at[it]).wait()
    pltpu.make_async_copy(mass_in, mass_in, mass_send).wait()


def solution(mesh):
    return local(mesh, mesh.shape["src"], mesh.shape["tgt"])


def local(mesh, n_src, n_tgt, comm=True):
    def per_device(xs, ys, a_mass, b_mass, s_region, t_region, allowed):
        width, n_i = xs.shape
        n_j = ys.shape[1]
        share = width // n_src
        tiles = n_i // TILE
        chips = n_tgt // 2
        piece = n_i // n_tgt
        vmem = pl.BlockSpec(memory_space=pltpu.VMEM)
        smem = pl.BlockSpec(memory_space=pltpu.SMEM)
        hbm = pl.BlockSpec(memory_space=pltpu.HBM)
        dma = pltpu.SemaphoreType.DMA

        def call(body, in_hbm, f_shape, g_shape, scratch, identity):
            return pl.pallas_call(
                functools.partial(body, n_src=n_src, n_tgt=n_tgt),
                out_shape=(
                    jax.ShapeDtypeStruct(f_shape, F32),
                    jax.ShapeDtypeStruct(g_shape, F32),
                    jax.ShapeDtypeStruct((share, n_j), F32),
                ),
                in_specs=[hbm if in_hbm else vmem] * 4 + [smem] * 3,
                out_specs=(vmem, vmem, vmem),
                scratch_shapes=scratch,
                compiler_params=pltpu.CompilerParams(
                    collective_id=identity if comm else None,
                    has_side_effects=comm,
                    vmem_limit_bytes=VMEM_MIB * 1024 * 1024,
                ),
            )(xs, ys, a_mass.reshape(f_shape), b_mass.reshape(g_shape), s_region, t_region, allowed)

        f, g, projected = call(
            functools.partial(kernel, comm=comm), True, (n_i // LANES, LANES), (n_j // LANES, LANES),
            [
                pltpu.VMEM((width, n_j), BF16),
                pltpu.VMEM((n_i // LANES, LANES), F32),
                pltpu.VMEM((n_j // LANES, LANES), F32),
                pltpu.VMEM((256, n_i), BF16),
                pltpu.VMEM((256, n_j), BF16),
                pltpu.VMEM((n_j, 256), BF16),
                pltpu.VMEM((n_i, 128), BF16),
                pltpu.VMEM((n_i // LANES, LANES), F32),
                pltpu.VMEM((n_j // LANES, LANES), F32),
                pltpu.VMEM((n_j, n_i), F32),
                pltpu.VMEM((n_j, LANES), F32),
                pltpu.VMEM((n_j, LANES), F32),
                pltpu.VMEM((n_i // LANES, LANES), F32),
                pltpu.VMEM((n_i // LANES, LANES), F32),
                pltpu.VMEM((ITERS, tiles, 2, 8, LANES), F32),
                pltpu.VMEM((ITERS, tiles, chips, 8, LANES), F32),
                pltpu.VMEM((ITERS, n_src, 8, LANES), F32),
                pltpu.VMEM((n_j, LANES), F32),
                pltpu.VMEM((n_src, share, n_j), F32),
                pltpu.VMEM((n_src, share, n_j), F32),
                dma((6,)),
                dma((ITERS, tiles)), dma((ITERS, tiles)), dma((ITERS, tiles)), dma((ITERS, tiles)),
                dma((ITERS,)), dma((ITERS,)), dma, dma,
            ],
            0,
        )
        f, g = f.reshape(n_i), g.reshape(n_j)
        if not comm:
            return f, g, projected

        def careful():
            f, g, projected = call(
                careful_kernel, False, (1, n_i), (1, n_j),
                [
                    pltpu.VMEM((256, n_i), BF16),
                    pltpu.VMEM((256, n_j), BF16),
                    pltpu.VMEM((n_i, 256), BF16),
                    pltpu.VMEM((n_j, 256), BF16),
                    pltpu.VMEM((ITERS, 1, n_i), F32),
                    pltpu.VMEM((ITERS, 1, n_j), F32),
                    pltpu.VMEM((n_src, share, n_j), F32),
                    pltpu.VMEM((ITERS, n_tgt - 1, 1, piece), F32),
                    pltpu.VMEM((ITERS, 1, n_i), F32),
                    pltpu.VMEM((ITERS, n_src - 1, 1, n_j), F32),
                    pltpu.VMEM((n_src - 1, share, n_j), F32),
                    dma((ITERS,)), dma((ITERS,)), dma((ITERS,)), dma((ITERS,)),
                    dma((ITERS,)), dma((ITERS,)), dma, dma,
                ],
                1,
            )
            return f.reshape(n_i), g.reshape(n_j), projected

        return lax.cond(jnp.isnan(g[0]), careful, lambda: (f, g, projected))

    placed = (P(None, "src"), P(None, "tgt"), P("src"), P("tgt"), P("src"), P("tgt"), P())
    return jax.shard_map(
        per_device,
        mesh=mesh,
        in_specs=placed,
        out_specs=(P("src"), P("tgt"), P("src", "tgt")),
        check_vma=False,
    )
```

time: 116 us -> 164 us (1.41)
  Pallas kernels: 108 us -> 158 us
  local copies, waits for them, and re-layouts: 6.52 us -> 3.63 us
    pallas_call x1 -> x2, Pallas kernels: 108 us -> 158 us  [call(): pl.pallas_call(functools.partial(body, n_src=n_src, n_tgt=n_tgt), out_sha...]
    unnamed x17, local copies, waits for them, and re-layouts: 6.52 us -> 3.12 us
where the time goes in v3:
time: 164 us; the launch traced here: 163 us
  Pallas kernels  158 us (96%)
  local copies, waits for them, and re-layouts  3.63 us (2%)
  between operations  2.02 us (1%)
    pallas_call x2, Pallas kernels, call(): pl.pallas_call(functools.partial(body, n_src=n_src, n_tgt=n_tgt), out_sha...  158 us

profile of v3, /device:TPU:2, one launch (start us, length us, event | category | flops | bytes accessed | tf_op | source)
XLA Modules:
  0.0 163.2 jit_solution(6008008518674634124)
XLA Ops:
  0.6 0.0 copy-start.4
  0.6 0.0 copy-start
  0.7 0.7 copy-done.4
  1.3 0.0 copy-start.1
  1.3 0.0 copy-start.2
  1.3 54.7 %shard_map.96 = (f32[32,128]{1,0:T(8,128)S(1)}, f32[8,128]{1,0:T(8,128)S(1)}, f32[8,1024]{1,0:T(8,128)S(1)}) custom-call(bf16[64,4096]{1,0:T(8,128)(2,1)} %xs_hbm.1, bf16[64,1024]{1,0:T(8,128)(2,1)} %ys_hbm.1, f32[32,128]{1,0:T(8,128)} %bitcast.9, f32[8,128]{1,0:T(8,128)S(1)} %bitcast.11, s32[4]{0:T(128)} %s_region.1, s32[2]{0:T(128)} %t_region.1, ...), custom_call_target="tpu_custom_call" | custom-call | tf_op jit(solution)/shard_map/pallas_call | solution.py:561
  56.0 0.0 copy-start.3
  56.0 0.5 slice.3
  57.8 0.0 copy-start.5
  57.8 0.0 copy-start.6
  57.8 0.0 copy-done
  57.9 0.0 copy-done.1
  57.9 0.0 copy-done.2
  57.9 0.0 copy-done.3
  57.9 0.6 copy-done.5
  58.5 0.0 copy-done.6
  58.5 102.8 %conditional.1 = (f32[1024]{0:T(1024)S(1)}, f32[8,1024]{1,0:T(8,128)S(1)}, f32[4096]{0:T(1024)S(1)}) conditional(s32[]{:T(128)} %bitcast.8, (f32[32,128]{1,0:T(8,128)S(1)}, f32[1024]{0:T(1024)S(1)}, f32[8,1024]{1,0:T(8,128)S(1)}) %tuple.30, (f32[4096]{0:T(1024)S(1)}, f32[1024]{0:T(1024)S(1)}, bf16[64,4096]{1,0:T(8,128)(2,1)S(1)}, ...), branch_computations={%region_0.0_spmd, %region_1.0_spmd} | conditional | bytes 24 | solution.py:633
  58.5 102.8 %branch_1_fun.1 = (f32[1,4096]{1,0:T(1,128)S(1)}, f32[1,1024]{1,0:T(1,128)S(1)}, f32[8,1024]{1,0:T(8,128)S(1)}) custom-call(bf16[64,4096]{1,0:T(8,128)(2,1)S(1)} %get-tuple-element.27.xs, bf16[64,1024]{1,0:T(8,128)(2,1)S(1)} %get-tuple-element.28.ys, f32[1,4096]{1,0:T(1,128)S(1)} %bitcast.10, f32[1,1024]{1,0:T(1,128)S(1)} %bitcast.12, ...), custom_call_target="tpu_custom_call" | custom-call | tf_op jit(solution)/shard_map/cond/branch_1_fun/pallas_call | solution.py:561
  161.4 0.6 copy.22
  162.0 0.6 copy.23
  162.6 0.6 copy.24
Async XLA Ops:
  0.6 0.7 copy-start.4
  0.6 57.2 %copy-start = (bf16[64,4096]{1,0:T(8,128)(2,1)S(1)}, bf16[64,4096]{1,0:T(8,128)(2,1)}, u32[]{:S(2)}) copy-start(bf16[64,4096]{1,0:T(8,128)(2,1)} %xs_hbm.1) | copy-start | bytes 1572868
  1.3 56.5 %copy-start.1 = (bf16[64,1024]{1,0:T(8,128)(2,1)S(1)}, bf16[64,1024]{1,0:T(8,128)(2,1)}, u32[]{:S(2)}) copy-start(bf16[64,1024]{1,0:T(8,128)(2,1)} %ys_hbm.1) | copy-start | bytes 393220
  1.3 56.6 %copy-start.2 = (f32[4096]{0:T(1024)S(1)}, f32[4096]{0:T(1024)}, u32[]{:S(2)}) copy-start(f32[4096]{0:T(1024)} %param.11) | copy-start | bytes 49156
  56.0 1.9 %copy-start.3 = (s32[16,16]{1,0:T(8,128)S(1)}, s32[16,16]{1,0:T(8,128)}, u32[]{:S(2)}) copy-start(s32[16,16]{1,0:T(8,128)} %allowed.1) | copy-start | bytes 3076
  57.8 0.7 copy-start.5
  57.8 0.7 copy-start.6

commit v4 on v3

--- a/solution.py
+++ b/solution.py
@@ -25,6 +25,8 @@
 TAIL = 128
 POT = TAIL + 32
 VMEM_MIB = 63
+SHIFT = 60.0
+LARGEST = 2.0**110
 F32 = jnp.float32
 BF16 = jnp.bfloat16
 
@@ -38,26 +40,6 @@
 
 def dot(a, b):
     return jnp.dot(a, b, preferred_element_type=F32)
-
-
-def block_lse(lhs, rhs):
-    peaks, sums = [], []
-    for at in range(0, lhs.shape[0], SUB):
-        scores = dot(lhs[at : at + SUB, :], rhs).reshape(SUB // 8, 8, rhs.shape[1])
-        peak = jnp.max(scores, axis=0)
-        peaks.append(peak)
-        sums.append(jnp.sum(jnp.exp2(scores - peak[None]), axis=0))
-    largest = functools.reduce(jnp.maximum, peaks)
-    summed = sum(total * jnp.exp2(peak - largest) for peak, total in zip(peaks, sums))
-    peak = jnp.max(largest, axis=0, keepdims=True)
-    return peak + jnp.log2(jnp.sum(summed * jnp.exp2(largest - peak), axis=0, keepdims=True))
-
-
-def joined(values, logs):
-    if not logs:
-        return jnp.sum(values, axis=0)
-    largest = jnp.max(values, axis=0)
-    return largest + jnp.log2(jnp.sum(jnp.exp2(values - largest[None]), axis=0))
 
 
 def or_nan(safe, value):
@@ -89,9 +71,9 @@
 
 
 def kernel(
-    xs_hbm, ys_hbm, a_hbm, b_hbm, s_region, t_region, allowed,
-    f_out, g_out, projected,
-    ys, a_mass, b_mass, x_aug, y_aug, y_t, x_t, x_term, y_term, coupling, w_col, acc, first_f, last_f,
+    xs_hbm, ys_hbm, a_hbm, b_hbm, s_hbm, t_hbm, allowed_hbm,
+    f_out, g_out, projected, b_copy, failed, s_copy, t_copy,
+    ys, a_mass, b_mass, s_region, t_region, allowed, x_aug, y_aug, y_t, x_t, y_term, coupling, w_col, acc, last_f,
     pair_in, row_in, col_in, numer, numer_t, mass_in,
     load_sem, pair_send, pair_recv, row_send, row_recv, col_send, col_recv, mass_send, mass_recv,
     *, n_src, n_tgt, comm,
@@ -119,7 +101,7 @@
         pltpu.make_async_copy(source, target, load_sem.at[k])
         for k, (source, target) in enumerate((
             (ys_hbm, ys), (b_hbm, b_mass), (xs_hbm, x_aug.at[0:64]), (xs_hbm, x_aug.at[64:128]),
-            (xs_hbm, x_aug.at[192:256]), (a_hbm, a_mass),
+            (xs_hbm, x_aug.at[192:256]), (a_hbm, a_mass), (s_hbm, s_region), (t_hbm, t_region), (allowed_hbm, allowed),
         ))
     ]
     for load in loads:
@@ -139,9 +121,12 @@
     def wait(ref, sem):
         pltpu.make_async_copy(ref, ref, sem).wait()
 
-    row = lax.broadcasted_iota(jnp.int32, (64, n_i), 0)
-    col = lax.broadcasted_iota(jnp.int32, (64, n_i), 1)
-    x_aug[TAIL : TAIL + 64, :] = jnp.where((row < 24) | (row - 24 == col // SB), 1.0, 0.0).astype(BF16)
+    row = lax.broadcasted_iota(jnp.int32, (32, n_i), 0)
+    col = lax.broadcasted_iota(jnp.int32, (32, n_i), 1)
+    x_aug[TAIL:POT, :] = jnp.where((row < 24) | (row - 24 == col // SB), 1.0, 0.0).astype(BF16)
+    x_aug[POT + 16 : POT + 32, :] = jnp.zeros((16, n_i), BF16)
+    for load in loads[:2] + loads[6:]:
+        load.wait()
     row = lax.broadcasted_iota(jnp.int32, (8, n_j), 0)
     col = lax.broadcasted_iota(jnp.int32, (8, n_j), 1)
     mask = jnp.zeros((8, n_j), F32)
@@ -153,8 +138,6 @@
     ones = jnp.where(row < 3, 1.0, 0.0)
     tail = [jnp.zeros((24, n_j), F32), mask, ones, jnp.zeros((24, n_j), F32)]
     y_aug[TAIL : TAIL + 64, :] = jnp.concatenate(tail, axis=0).astype(BF16)
-    for load in loads[:2]:
-        load.wait()
     y_wide = ys[...].astype(F32)
     y_parts = split3(y_wide * (2.0 * KAPPA / width))
     y_aug[0:64, :] = y_parts[0].astype(BF16)
@@ -166,9 +149,18 @@
     for c in range(n_j // LANES):
         y_term[c : c + 1, :] = y_squares[:, c * LANES : (c + 1) * LANES]
     b_log = jnp.log2(b_mass[...])
-    put_potential(b_log + y_term[...], y_t)
-    for load in loads[2:]:
+    put_potential(b_log + y_term[...] + SHIFT, y_t)
+    for load in loads[2:6]:
         load.wait()
+    row16 = lax.broadcasted_iota(jnp.int32, (16, TILE), 0)
+    for s in range(tiles):
+        at = slice(s * TILE, (s + 1) * TILE)
+        x_wide = x_aug[0:64, at].astype(F32)
+        x_term = jnp.sum(x_wide * x_wide, axis=0, keepdims=True) * (-KAPPA / width)
+        tail = jnp.zeros((16, TILE), F32)
+        for k, part in enumerate(split3(x_term)):
+            tail = jnp.where(row16 == k, part, tail)
+        x_aug[POT : POT + 16, at] = tail.astype(BF16)
 
     def pair_send_tile(it, s):
         if comm:
@@ -178,7 +170,7 @@
     def chip_send_tile(it, s):
         if comm:
             wait(pair_in.at[it, s, 0], pair_recv.at[it, s])
-        row_in[it, s, my_chip] = joined(pair_in[it, s], it == 0)
+        row_in[it, s, my_chip] = pair_in[it, s, 0] + pair_in[it, s, 1]
         if comm:
             mine = row_in.at[it, s, my_chip]
             for offset in chip_order:
@@ -187,22 +179,20 @@
     def row_total(it, s):
         if comm:
             wait(row_in.at[it, s, pl.ds(0, chips - 1)], row_recv.at[it, s])
-        return joined(row_in[it, s], it == 0)
+        return jnp.sum(row_in[it, s], axis=0)
 
     def tile_of(s):
         return slice(s * 8, (s + 1) * 8)
 
     def source_factor(it, s):
         total = row_total(it, s)
-        a_log = jnp.log2(a_mass[tile_of(s), :])
-        first = first_f[tile_of(s), :]
-        f2 = -DAMPING * (jnp.log2(total) - a_log - first)
-        safe = (total >= 2.0**-28) & (jnp.abs(f2 - first) <= 30.0)
-        if it > 1:
+        f2 = -DAMPING * (jnp.log2(total) - SHIFT)
+        safe = (total >= 2.0 ** (SHIFT - 95.0)) & (total <= LARGEST)
+        if it == ITERS - 1:
             safe &= jnp.abs(f2 - last_f[tile_of(s), :]) <= 8.0
         f2 = or_nan(safe, f2)
         last_f[tile_of(s), :] = f2
-        return jnp.exp2(f2 - first), f2
+        return jnp.exp2(f2 + jnp.log2(a_mass[tile_of(s), :])), f2
 
     def target_total(it):
         for r in range(8):
@@ -215,17 +205,26 @@
             wait(col_in.at[it, pl.ds(0, n_src - 1)], col_recv.at[it])
         return jnp.sum(col_in[it], axis=0)
 
+    def target_potential(total):
+        return -DAMPING * (jnp.log2(total) - SHIFT - b_log)
+
     def target_factor(it):
         total = target_total(it)
-        g2 = -DAMPING * (jnp.log2(total) - b_log)
-        w = jnp.exp2(or_nan(total >= 2.0 ** (-60.0 if it == 0 else -50.0), g2))
+        safe = (total >= 2.0 ** (SHIFT - 49.0)) & (total <= LARGEST)
+        w = jnp.exp2(or_nan(safe, target_potential(total)))
         for r in range(8):
             w_col[r * LANES : (r + 1) * LANES, :] = jnp.broadcast_to(w[r : r + 1, :], (LANES, LANES)).T
 
     for s in range(tiles):
         for c in range(TILE // WIDE):
-            at = s * TILE + c * WIDE
-            value = block_lse(y_t, x_aug[:, at : at + WIDE])
+            at = slice(s * TILE + c * WIDE, s * TILE + (c + 1) * WIDE)
+            rhs = x_aug[:, at]
+            sums = jnp.zeros((8, WIDE), F32)
+            for j in range(0, n_j, SUB):
+                block = jnp.exp2(dot(y_t[j : j + SUB, :], rhs))
+                coupling[j : j + SUB, at] = block
+                sums += jnp.sum(block.reshape(SUB // 8, 8, WIDE), axis=0)
+            value = jnp.sum(sums, axis=0, keepdims=True)
             for h in range(WIDE // LANES):
                 r = c * (WIDE // LANES) + h
                 pair_in[0, s, my_core, r : r + 1, :] = value[:, h * LANES : (h + 1) * LANES]
@@ -234,35 +233,9 @@
         pair_send_tile(0, s)
         if s > 0:
             chip_send_tile(0, s - 1)
-    x_wide = x_aug[0:64, :].astype(F32)
-    x_squares = jnp.sum(x_wide * x_wide, axis=0, keepdims=True) * (-KAPPA / width)
-    for c in range(n_i // LANES):
-        x_term[c : c + 1, :] = x_squares[:, c * LANES : (c + 1) * LANES]
     chip_send_tile(0, tiles - 1)
     for c in range(n_i // WIDE):
         x_t[c * WIDE : (c + 1) * WIDE, :] = x_aug[0:128, c * WIDE : (c + 1) * WIDE].T
-
-    row16 = lax.broadcasted_iota(jnp.int32, (16, TILE), 0)
-    for s in range(tiles):
-        whole = row_total(0, s) + x_term[tile_of(s), :]
-        a_log = jnp.log2(a_mass[tile_of(s), :])
-        scale = a_log + (1.0 - DAMPING) * whole
-        f2 = or_nan(jnp.abs(scale) <= 30.0, -DAMPING * whole)
-        first_f[tile_of(s), :] = f2
-        last_f[tile_of(s), :] = f2
-        score = jnp.zeros((16, TILE), F32)
-        for k, part in enumerate(split3(a_log + f2 + x_term[tile_of(s), :])):
-            score = jnp.where(row16 == k, lane_row(part), score)
-        x_aug[POT : POT + 16, s * TILE : (s + 1) * TILE] = score.astype(BF16)
-        for c in range(TILE // WIDE):
-            at = slice(s * TILE + c * WIDE, s * TILE + (c + 1) * WIDE)
-            rhs = x_aug[:, at]
-            for j in range(0, n_j, SUB):
-                block = jnp.exp2(dot(y_t[j : j + SUB, :], rhs))
-                coupling[j : j + SUB, at] = block
-                part = fold_lanes(block)
-                acc[j : j + SUB, :] = part if s == 0 and c == 0 else acc[j : j + SUB, :] + part
-    target_factor(0)
 
     def row_sweep(it):
         for s in range(tiles):
@@ -275,11 +248,14 @@
             for r in range(8):
                 pair_in[it, s, my_core, r : r + 1, :] = value[:, r * LANES : (r + 1) * LANES]
             pair_send_tile(it, s)
-        for s in range(tiles):
+            if s > 1:
+                chip_send_tile(it, s - 2)
+        for s in range(tiles - 2, tiles):
             chip_send_tile(it, s)
 
-    for it in range(1, ITERS - 1):
-        row_sweep(it)
+    for it in range(ITERS - 1):
+        if it > 0:
+            row_sweep(it)
         for s in range(tiles):
             factor = lane_row(source_factor(it, s)[0])
             for j in range(0, n_j, ROWS):
@@ -298,7 +274,8 @@
             rows = slice(j, j + SUB)
             weight = coupling[rows, s * TILE : (s + 1) * TILE] * factor
             part = fold_lanes(weight)
-            product = dot(weight.astype(BF16), x_t[s * TILE : (s + 1) * TILE, :])
+            latent = x_t[s * TILE : (s + 1) * TILE, :]
+            product = dot(weight.astype(BF16), latent)
             if s > 0:
                 part += acc[rows, :]
                 product += numer[rows, :]
@@ -318,7 +295,14 @@
                         mass_send, mass_recv, (owner, my_tgt),
                     )
     total = target_total(last)
-    g_out[...] = (-DAMPING / KAPPA) * (jnp.log2(total) - b_log)
+    g2 = target_potential(total)
+    g_out[...] = g2 * (1.0 / KAPPA)
+    for k in range(n_i // SB):
+        s_copy[k] = s_region[k]
+    for k in range(n_j // TB):
+        t_copy[k] = t_region[k]
+    b_copy[...] = b_mass[...]
+    failed[0] = jnp.sum(jnp.where(g2 == g2, 0, 1))
     if comm:
         wait(mass_in.at[pl.ds(0, n_src - 1)], mass_recv)
     projected[...] = jnp.sum(mass_in[...], axis=0) / lane_row(total)
@@ -557,16 +541,23 @@
         hbm = pl.BlockSpec(memory_space=pltpu.HBM)
         dma = pltpu.SemaphoreType.DMA
 
-        def call(body, in_hbm, f_shape, g_shape, scratch, identity):
+        def call(body, first, b_mass, s_region, t_region, f_shape, g_shape, scratch, identity):
+            spare = (
+                jax.ShapeDtypeStruct(g_shape, F32),
+                jax.ShapeDtypeStruct((1,), jnp.int32),
+                jax.ShapeDtypeStruct(s_region.shape, jnp.int32),
+                jax.ShapeDtypeStruct(t_region.shape, jnp.int32),
+            )
             return pl.pallas_call(
                 functools.partial(body, n_src=n_src, n_tgt=n_tgt),
                 out_shape=(
                     jax.ShapeDtypeStruct(f_shape, F32),
                     jax.ShapeDtypeStruct(g_shape, F32),
                     jax.ShapeDtypeStruct((share, n_j), F32),
-                ),
-                in_specs=[hbm if in_hbm else vmem] * 4 + [smem] * 3,
-                out_specs=(vmem, vmem, vmem),
+                )
+                + spare * first,
+                in_specs=[hbm] * 7 if first else [vmem] * 4 + [smem] * 3,
+                out_specs=(vmem, vmem, vmem) + (vmem, smem, smem, smem) * first,
                 scratch_shapes=scratch,
                 compiler_params=pltpu.CompilerParams(
                     collective_id=identity if comm else None,
@@ -575,22 +566,23 @@
                 ),
             )(xs, ys, a_mass.reshape(f_shape), b_mass.reshape(g_shape), s_region, t_region, allowed)
 
-        f, g, projected = call(
-            functools.partial(kernel, comm=comm), True, (n_i // LANES, LANES), (n_j // LANES, LANES),
+        f, g, projected, b_copy, failed, s_copy, t_copy = call(
+            functools.partial(kernel, comm=comm), 1, b_mass, s_region, t_region, (n_i // LANES, LANES), (n_j // LANES, LANES),
             [
                 pltpu.VMEM((width, n_j), BF16),
                 pltpu.VMEM((n_i // LANES, LANES), F32),
                 pltpu.VMEM((n_j // LANES, LANES), F32),
+                pltpu.SMEM(s_region.shape, jnp.int32),
+                pltpu.SMEM(t_region.shape, jnp.int32),
+                pltpu.SMEM(allowed.shape, jnp.int32),
                 pltpu.VMEM((256, n_i), BF16),
                 pltpu.VMEM((256, n_j), BF16),
                 pltpu.VMEM((n_j, 256), BF16),
                 pltpu.VMEM((n_i, 128), BF16),
-                pltpu.VMEM((n_i // LANES, LANES), F32),
                 pltpu.VMEM((n_j // LANES, LANES), F32),
                 pltpu.VMEM((n_j, n_i), F32),
                 pltpu.VMEM((n_j, LANES), F32),
                 pltpu.VMEM((n_j, LANES), F32),
-                pltpu.VMEM((n_i // LANES, LANES), F32),
                 pltpu.VMEM((n_i // LANES, LANES), F32),
                 pltpu.VMEM((ITERS, tiles, 2, 8, LANES), F32),
                 pltpu.VMEM((ITERS, tiles, chips, 8, LANES), F32),
@@ -598,7 +590,7 @@
                 pltpu.VMEM((n_j, LANES), F32),
                 pltpu.VMEM((n_src, share, n_j), F32),
                 pltpu.VMEM((n_src, share, n_j), F32),
-                dma((6,)),
+                dma((9,)),
                 dma((ITERS, tiles)), dma((ITERS, tiles)), dma((ITERS, tiles)), dma((ITERS, tiles)),
                 dma((ITERS,)), dma((ITERS,)), dma, dma,
             ],
@@ -610,7 +602,7 @@
 
         def careful():
             f, g, projected = call(
-                careful_kernel, False, (1, n_i), (1, n_j),
+                careful_kernel, 0, b_copy, s_copy, t_copy, (1, n_i), (1, n_j),
                 [
                     pltpu.VMEM((256, n_i), BF16),
                     pltpu.VMEM((256, n_j), BF16),
@@ -630,7 +622,7 @@
             )
             return f.reshape(n_i), g.reshape(n_j), projected
 
-        return lax.cond(jnp.isnan(g[0]), careful, lambda: (f, g, projected))
+        return lax.cond(failed[0] > 0, careful, lambda: (f, g, projected))
 
     placed = (P(None, "src"), P(None, "tgt"), P("src"), P("tgt"), P("src"), P("tgt"), P())
     return jax.shard_map(

time: 164 us -> 160 us (0.976)
  local copies, waits for them, and re-layouts: 3.63 us -> 1.83 us
where the time goes in v4:
time: 160 us
  Pallas kernels  157 us (98%)
  local copies, waits for them, and re-layouts  1.83 us (1%)
    pallas_call x2, Pallas kernels, call(): pl.pallas_call(functools.partial(body, n_src=n_src, n_tgt=n_tgt), out_sha...  157 us

profile of v4, /device:TPU:2, one launch (start us, length us, event | category | flops | bytes accessed | tf_op | source)
XLA Modules:
  0.0 160.3 jit_solution(7438673092896849292)
XLA Ops:
  0.6 0.0 copy-start
  0.6 0.0 copy-start.1
  0.7 0.0 copy-start.3
  0.7 53.2 %shard_map.98 = (f32[32,128]{1,0:T(8,128)S(1)}, f32[8,128]{1,0:T(8,128)S(1)}, f32[8,1024]{1,0:T(8,128)S(1)}, f32[8,128]{1,0:T(8,128)S(1)}, s32[1]{0:T(128)}, /*index=5*/s32[4]{0:T(128)S(1)}, s32[2]{0:T(128)S(1)}) custom-call(bf16[64,4096]{1,0:T(8,128)(2,1)} %xs_hbm.1, bf16[64,1024]{1,0:T(8,128)(2,1)} %ys_hbm.1, f32[32,128]{1,0:T(8,128)} %bitcast.9, ...), custom_call_target="tpu_custom_call" | custom-call | tf_op jit(solution)/shard_map/pallas_call | solution.py:551
  53.9 0.0 copy-start.2
  54.6 0.0 copy-done
  54.6 0.0 copy-done.1
  54.6 0.0 copy-done.3
  54.6 0.0 copy-done.2
  54.7 103.8 %conditional.1 = (f32[8,1024]{1,0:T(8,128)S(1)}, f32[4096]{0:T(1024)S(1)}, f32[1024]{0:T(1024)S(1)}) conditional(s32[]{:T(128)} %bitcast.8, (f32[32,128]{1,0:T(8,128)S(1)}, f32[8,128]{1,0:T(8,128)S(1)}, f32[8,1024]{1,0:T(8,128)S(1)}) %tuple.24, (f32[4096]{0:T(1024)S(1)}, f32[8,128]{1,0:T(8,128)S(1)}, bf16[64,4096]{1,0:T(8,128)(2,1)S(1)}, ...), branch_computations={%region_0.0_spmd, %region_1.0_spmd} | conditional | bytes 24 | solution.py:625
  54.7 103.8 %branch_1_fun.1 = (f32[1,4096]{1,0:T(1,128)S(1)}, f32[1,1024]{1,0:T(1,128)S(1)}, f32[8,1024]{1,0:T(8,128)S(1)}) custom-call(bf16[64,4096]{1,0:T(8,128)(2,1)S(1)} %get-tuple-element.28.xs, bf16[64,1024]{1,0:T(8,128)(2,1)S(1)} %get-tuple-element.29.ys, f32[1,4096]{1,0:T(1,128)S(1)} %bitcast.10, f32[1,1024]{1,0:T(1,128)S(1)} %bitcast.14, ...), custom_call_target="tpu_custom_call" | custom-call | tf_op jit(solution)/shard_map/cond/branch_1_fun/pallas_call | solution.py:551
  158.5 0.6 copy.25
  159.1 0.6 copy.26
  159.7 0.6 copy.27
Async XLA Ops:
  0.6 54.0 %copy-start = (bf16[64,4096]{1,0:T(8,128)(2,1)S(1)}, bf16[64,4096]{1,0:T(8,128)(2,1)}, u32[]{:S(2)}) copy-start(bf16[64,4096]{1,0:T(8,128)(2,1)} %xs_hbm.1) | copy-start | bytes 1572868
  0.6 54.0 %copy-start.1 = (bf16[64,1024]{1,0:T(8,128)(2,1)S(1)}, bf16[64,1024]{1,0:T(8,128)(2,1)}, u32[]{:S(2)}) copy-start(bf16[64,1024]{1,0:T(8,128)(2,1)} %ys_hbm.1) | copy-start | bytes 393220
  0.7 54.0 %copy-start.3 = (s32[16,16]{1,0:T(8,128)S(1)}, s32[16,16]{1,0:T(8,128)}, u32[]{:S(2)}) copy-start(s32[16,16]{1,0:T(8,128)} %allowed_hbm.1) | copy-start | bytes 3076
  53.9 0.7 copy-start.2

commit v5 on v4

--- a/solution.py
+++ b/solution.py
@@ -74,13 +74,14 @@
     xs_hbm, ys_hbm, a_hbm, b_hbm, s_hbm, t_hbm, allowed_hbm,
     f_out, g_out, projected, b_copy, failed, s_copy, t_copy,
     ys, a_mass, b_mass, s_region, t_region, allowed, x_aug, y_aug, y_t, x_t, y_term, coupling, w_col, acc, last_f,
-    pair_in, row_in, col_in, numer, numer_t, mass_in,
-    load_sem, pair_send, pair_recv, row_send, row_recv, col_send, col_recv, mass_send, mass_recv,
+    part_own, part_sib, pair_in, row_in, total_own, total_in, col_in, numer, numer_t, mass_in,
+    load_sem, pair_sent, pair_recv, row_sent, row_recv, total_sent, total_recv, col_send, col_recv, mass_send, mass_recv,
     *, n_src, n_tgt, comm,
 ):
     width, n_j = ys.shape
     n_i = x_aug.shape[1]
     tiles = n_i // TILE
+    half = tiles // 2
     chips = n_tgt // 2
     share = width // n_src
     src_order, chip_order = farthest_first(n_src, n_tgt)
@@ -162,30 +163,47 @@
             tail = jnp.where(row16 == k, part, tail)
         x_aug[POT : POT + 16, at] = tail.astype(BF16)
 
-    def pair_send_tile(it, s):
-        if comm:
-            mine = pair_in.at[it, s, my_core]
-            send(mine, mine, pair_send.at[it, s], pair_recv.at[it, s], sibling)
-
-    def chip_send_tile(it, s):
-        if comm:
-            wait(pair_in.at[it, s, 0], pair_recv.at[it, s])
-        row_in[it, s, my_chip] = pair_in[it, s, 0] + pair_in[it, s, 1]
-        if comm:
-            mine = row_in.at[it, s, my_chip]
-            for offset in chip_order:
-                send(mine, mine, row_send.at[it, s], row_recv.at[it, s], chip_peer(offset))
-
-    def row_total(it, s):
-        if comm:
-            wait(row_in.at[it, s, pl.ds(0, chips - 1)], row_recv.at[it, s])
-        return jnp.sum(row_in[it, s], axis=0)
-
-    def tile_of(s):
-        return slice(s * 8, (s + 1) * 8)
-
-    def source_factor(it, s):
-        total = row_total(it, s)
+    own_tiles = [my_core * half + q for q in range(half)]
+    sib_tiles = [(1 - my_core) * half + q for q in range(half)]
+
+    def tile_of(tile):
+        return pl.ds(pl.multiple_of(tile * 8, 8), 8)
+
+    def cells_of(tile):
+        return pl.ds(pl.multiple_of(tile * TILE, TILE), TILE)
+
+    def row_parts(it, sweep):
+        for q, tile in enumerate(sib_tiles):
+            sweep(tile, part_sib.at[it, q])
+            if comm and it == 0 and q == 0:
+                pl.semaphore_wait(barrier, len(peers))
+            if comm:
+                send(part_sib.at[it, q], pair_in.at[it, q], pair_sent.at[it, q], pair_recv.at[it, q], sibling)
+        for q, tile in enumerate(own_tiles):
+            sweep(tile, part_own.at[q])
+            if comm:
+                wait(pair_in.at[it, q], pair_recv.at[it, q])
+            row_in[it, q, my_chip] = part_own[q] + pair_in[it, q]
+            if comm:
+                mine = row_in.at[it, q, my_chip]
+                for offset in chip_order:
+                    send(mine, mine, row_sent.at[it, q], row_recv.at[it, q], chip_peer(offset))
+
+    def row_totals(it):
+        for q, tile in enumerate(own_tiles):
+            if comm:
+                wait(row_in.at[it, q, pl.ds(0, chips - 1)], row_recv.at[it, q])
+            total = jnp.sum(row_in[it, q], axis=0)
+            total_own[it, q] = total
+            if comm:
+                send(total_own.at[it, q], total_in.at[it, q], total_sent.at[it, q], total_recv.at[it, q], sibling)
+            yield q, tile, total
+        for q, tile in enumerate(sib_tiles):
+            if comm:
+                wait(total_in.at[it, q], total_recv.at[it, q])
+            yield half + q, tile, total_in[it, q]
+
+    def source_factor(it, s, total):
         f2 = -DAMPING * (jnp.log2(total) - SHIFT)
         safe = (total >= 2.0 ** (SHIFT - 95.0)) & (total <= LARGEST)
         if it == ITERS - 1:
@@ -215,9 +233,9 @@
         for r in range(8):
             w_col[r * LANES : (r + 1) * LANES, :] = jnp.broadcast_to(w[r : r + 1, :], (LANES, LANES)).T
 
-    for s in range(tiles):
+    def first_row_sweep(tile, out):
         for c in range(TILE // WIDE):
-            at = slice(s * TILE + c * WIDE, s * TILE + (c + 1) * WIDE)
+            at = pl.ds(pl.multiple_of(tile * TILE + c * WIDE, WIDE), WIDE)
             rhs = x_aug[:, at]
             sums = jnp.zeros((8, WIDE), F32)
             for j in range(0, n_j, SUB):
@@ -227,61 +245,50 @@
             value = jnp.sum(sums, axis=0, keepdims=True)
             for h in range(WIDE // LANES):
                 r = c * (WIDE // LANES) + h
-                pair_in[0, s, my_core, r : r + 1, :] = value[:, h * LANES : (h + 1) * LANES]
-        if comm and s == 0:
-            pl.semaphore_wait(barrier, len(peers))
-        pair_send_tile(0, s)
-        if s > 0:
-            chip_send_tile(0, s - 1)
-    chip_send_tile(0, tiles - 1)
+                out[r : r + 1, :] = value[:, h * LANES : (h + 1) * LANES]
+
+    row_parts(0, first_row_sweep)
     for c in range(n_i // WIDE):
         x_t[c * WIDE : (c + 1) * WIDE, :] = x_aug[0:128, c * WIDE : (c + 1) * WIDE].T
 
-    def row_sweep(it):
-        for s in range(tiles):
-            sums = jnp.zeros((8, TILE), F32)
-            for j in range(0, n_j, ROWS):
-                w = jnp.concatenate([w_col[j : j + ROWS, :]] * (TILE // LANES), axis=1)
-                block = coupling[j : j + ROWS, s * TILE : (s + 1) * TILE] * w
-                sums += jnp.sum(block.reshape(ROWS // 8, 8, TILE), axis=0)
-            value = jnp.sum(sums, axis=0, keepdims=True)
-            for r in range(8):
-                pair_in[it, s, my_core, r : r + 1, :] = value[:, r * LANES : (r + 1) * LANES]
-            pair_send_tile(it, s)
-            if s > 1:
-                chip_send_tile(it, s - 2)
-        for s in range(tiles - 2, tiles):
-            chip_send_tile(it, s)
+    def row_sweep(tile, out):
+        sums = jnp.zeros((8, TILE), F32)
+        for j in range(0, n_j, ROWS):
+            w = jnp.concatenate([w_col[j : j + ROWS, :]] * (TILE // LANES), axis=1)
+            block = coupling[j : j + ROWS, cells_of(tile)] * w
+            sums += jnp.sum(block.reshape(ROWS // 8, 8, TILE), axis=0)
+        value = jnp.sum(sums, axis=0, keepdims=True)
+        for r in range(8):
+            out[r : r + 1, :] = value[:, r * LANES : (r + 1) * LANES]
 
     for it in range(ITERS - 1):
         if it > 0:
-            row_sweep(it)
-        for s in range(tiles):
-            factor = lane_row(source_factor(it, s)[0])
+            row_parts(it, row_sweep)
+        for place, tile, sums in row_totals(it):
+            factor = lane_row(source_factor(it, tile, sums)[0])
             for j in range(0, n_j, ROWS):
-                block = coupling[j : j + ROWS, s * TILE : (s + 1) * TILE] * factor
+                block = coupling[j : j + ROWS, cells_of(tile)] * factor
                 part = fold_lanes(block)
-                acc[j : j + ROWS, :] = part if s == 0 else acc[j : j + ROWS, :] + part
+                acc[j : j + ROWS, :] = part if place == 0 else acc[j : j + ROWS, :] + part
         target_factor(it)
 
     last = ITERS - 1
-    row_sweep(last)
-    for s in range(tiles):
-        factor, f2 = source_factor(last, s)
-        f_out[tile_of(s), :] = f2 * (1.0 / KAPPA)
+    row_parts(last, row_sweep)
+    for place, tile, sums in row_totals(last):
+        factor, f2 = source_factor(last, tile, sums)
+        f_out[tile_of(tile), :] = f2 * (1.0 / KAPPA)
         factor = lane_row(factor)
         for j in range(0, n_j, SUB):
             rows = slice(j, j + SUB)
-            weight = coupling[rows, s * TILE : (s + 1) * TILE] * factor
+            weight = coupling[rows, cells_of(tile)] * factor
             part = fold_lanes(weight)
-            latent = x_t[s * TILE : (s + 1) * TILE, :]
-            product = dot(weight.astype(BF16), latent)
-            if s > 0:
+            product = dot(weight.astype(BF16), x_t[cells_of(tile), :])
+            if place > 0:
                 part += acc[rows, :]
                 product += numer[rows, :]
             acc[rows, :] = part
             numer[rows, :] = product
-            if s < tiles - 1:
+            if place < tiles - 1:
                 continue
             flat = product.T
             for d in range(n_src):
@@ -309,9 +316,10 @@
 
     if comm:
         for it in range(ITERS):
-            for s in range(tiles):
-                wait(pair_in.at[it, s, 0], pair_send.at[it, s])
-                wait(row_in.at[it, s, pl.ds(0, chips - 1)], row_send.at[it, s])
+            for q in range(half):
+                wait(pair_in.at[it, q], pair_sent.at[it, q])
+                wait(row_in.at[it, q, pl.ds(0, chips - 1)], row_sent.at[it, q])
+                wait(total_in.at[it, q], total_sent.at[it, q])
             wait(col_in.at[it, pl.ds(0, n_src - 1)], col_send.at[it])
         wait(mass_in.at[pl.ds(0, n_src - 1)], mass_send)
 
@@ -534,6 +542,7 @@
         n_j = ys.shape[1]
         share = width // n_src
         tiles = n_i // TILE
+        half = tiles // 2
         chips = n_tgt // 2
         piece = n_i // n_tgt
         vmem = pl.BlockSpec(memory_space=pltpu.VMEM)
@@ -584,14 +593,18 @@
                 pltpu.VMEM((n_j, LANES), F32),
                 pltpu.VMEM((n_j, LANES), F32),
                 pltpu.VMEM((n_i // LANES, LANES), F32),
-                pltpu.VMEM((ITERS, tiles, 2, 8, LANES), F32),
-                pltpu.VMEM((ITERS, tiles, chips, 8, LANES), F32),
+                pltpu.VMEM((half, 8, LANES), F32),
+                pltpu.VMEM((ITERS, half, 8, LANES), F32),
+                pltpu.VMEM((ITERS, half, 8, LANES), F32),
+                pltpu.VMEM((ITERS, half, chips, 8, LANES), F32),
+                pltpu.VMEM((ITERS, half, 8, LANES), F32),
+                pltpu.VMEM((ITERS, half, 8, LANES), F32),
                 pltpu.VMEM((ITERS, n_src, 8, LANES), F32),
                 pltpu.VMEM((n_j, LANES), F32),
                 pltpu.VMEM((n_src, share, n_j), F32),
                 pltpu.VMEM((n_src, share, n_j), F32),
                 dma((9,)),
-                dma((ITERS, tiles)), dma((ITERS, tiles)), dma((ITERS, tiles)), dma((ITERS, tiles)),
+                *[dma((ITERS, half))] * 6,
                 dma((ITERS,)), dma((ITERS,)), dma, dma,
             ],
             0,

time: 160 us -> 160 us (level)
  no operation moved by 1% of the time
where the time goes in v5:
time: 160 us; the launch traced here: 159 us
  Pallas kernels  156 us (98%)
  local copies, waits for them, and re-layouts  1.83 us (1%)
    pallas_call x2, Pallas kernels, call(): pl.pallas_call(functools.partial(body, n_src=n_src, n_tgt=n_tgt), out_sha...  156 us

profile of v5, /device:TPU:2, one launch (start us, length us, event | category | flops | bytes accessed | tf_op | source)
XLA Modules:
  0.0 158.9 jit_solution(3145733743246318534)
XLA Ops:
  0.6 0.0 copy-start
  0.6 0.0 copy-start.1
  0.7 0.0 copy-start.3
  0.7 52.6 %shard_map.98 = (f32[32,128]{1,0:T(8,128)S(1)}, f32[8,128]{1,0:T(8,128)S(1)}, f32[8,1024]{1,0:T(8,128)S(1)}, f32[8,128]{1,0:T(8,128)S(1)}, s32[1]{0:T(128)}, /*index=5*/s32[4]{0:T(128)S(1)}, s32[2]{0:T(128)S(1)}) custom-call(bf16[64,4096]{1,0:T(8,128)(2,1)} %xs_hbm.1, bf16[64,1024]{1,0:T(8,128)(2,1)} %ys_hbm.1, f32[32,128]{1,0:T(8,128)} %bitcast.9, ...), custom_call_target="tpu_custom_call" | custom-call | tf_op jit(solution)/shard_map/pallas_call | solution.py:560
  53.3 0.0 copy-start.2
  54.0 0.0 copy-done
  54.0 0.0 copy-done.1
  54.0 0.0 copy-done.3
  54.0 0.0 copy-done.2
  54.1 103.0 %conditional.1 = (f32[8,1024]{1,0:T(8,128)S(1)}, f32[4096]{0:T(1024)S(1)}, f32[1024]{0:T(1024)S(1)}) conditional(s32[]{:T(128)} %bitcast.8, (f32[32,128]{1,0:T(8,128)S(1)}, f32[8,128]{1,0:T(8,128)S(1)}, f32[8,1024]{1,0:T(8,128)S(1)}) %tuple.24, (f32[4096]{0:T(1024)S(1)}, f32[8,128]{1,0:T(8,128)S(1)}, bf16[64,4096]{1,0:T(8,128)(2,1)S(1)}, ...), branch_computations={%region_0.0_spmd, %region_1.0_spmd} | conditional | bytes 24 | solution.py:638
  54.1 103.0 %branch_1_fun.1 = (f32[1,4096]{1,0:T(1,128)S(1)}, f32[1,1024]{1,0:T(1,128)S(1)}, f32[8,1024]{1,0:T(8,128)S(1)}) custom-call(bf16[64,4096]{1,0:T(8,128)(2,1)S(1)} %get-tuple-element.28.xs, bf16[64,1024]{1,0:T(8,128)(2,1)S(1)} %get-tuple-element.29.ys, f32[1,4096]{1,0:T(1,128)S(1)} %bitcast.10, f32[1,1024]{1,0:T(1,128)S(1)} %bitcast.14, ...), custom_call_target="tpu_custom_call" | custom-call | tf_op jit(solution)/shard_map/cond/branch_1_fun/pallas_call | solution.py:560
  157.1 0.6 copy.25
  157.7 0.6 copy.26
  158.3 0.6 copy.27
Async XLA Ops:
  0.6 53.4 %copy-start = (bf16[64,4096]{1,0:T(8,128)(2,1)S(1)}, bf16[64,4096]{1,0:T(8,128)(2,1)}, u32[]{:S(2)}) copy-start(bf16[64,4096]{1,0:T(8,128)(2,1)} %xs_hbm.1) | copy-start | bytes 1572868
  0.6 53.4 %copy-start.1 = (bf16[64,1024]{1,0:T(8,128)(2,1)S(1)}, bf16[64,1024]{1,0:T(8,128)(2,1)}, u32[]{:S(2)}) copy-start(bf16[64,1024]{1,0:T(8,128)(2,1)} %ys_hbm.1) | copy-start | bytes 393220
  0.7 53.4 %copy-start.3 = (s32[16,16]{1,0:T(8,128)S(1)}, s32[16,16]{1,0:T(8,128)}, u32[]{:S(2)}) copy-start(s32[16,16]{1,0:T(8,128)} %allowed_hbm.1) | copy-start | bytes 3076
  53.3 0.7 copy-start.2

commit v6 on v5

--- a/solution.py
+++ b/solution.py
@@ -18,7 +18,7 @@
 FORBID = -(2.0**100)
 MESH = pl.DeviceIdType.MESH
 WIDE = 256
-SUB = 256
+SUB = 512
 ROWS = 32
 LANES = 128
 TILE = 1024

time: 160 us -> 160 us (level)
  no operation moved by 1% of the time
where the time goes in v6:
time: 160 us; the launch traced here: 159 us
  Pallas kernels  156 us (98%)
  local copies, waits for them, and re-layouts  1.83 us (1%)
    pallas_call x2, Pallas kernels, call(): pl.pallas_call(functools.partial(body, n_src=n_src, n_tgt=n_tgt), out_sha...  156 us

profile of v6, /device:TPU:2, one launch (start us, length us, event | category | flops | bytes accessed | tf_op | source)
XLA Modules:
  0.0 159.5 jit_solution(14541099122176457239)
XLA Ops:
  0.6 0.0 copy-start
  0.6 0.0 copy-start.1
  0.7 0.0 copy-start.3
  0.7 52.7 %shard_map.98 = (f32[32,128]{1,0:T(8,128)S(1)}, f32[8,128]{1,0:T(8,128)S(1)}, f32[8,1024]{1,0:T(8,128)S(1)}, f32[8,128]{1,0:T(8,128)S(1)}, s32[1]{0:T(128)}, /*index=5*/s32[4]{0:T(128)S(1)}, s32[2]{0:T(128)S(1)}) custom-call(bf16[64,4096]{1,0:T(8,128)(2,1)} %xs_hbm.1, bf16[64,1024]{1,0:T(8,128)(2,1)} %ys_hbm.1, f32[32,128]{1,0:T(8,128)} %bitcast.9, ...), custom_call_target="tpu_custom_call" | custom-call | tf_op jit(solution)/shard_map/pallas_call | solution.py:560
  53.3 0.0 copy-start.2
  54.0 0.0 copy-done
  54.1 0.0 copy-done.1
  54.1 0.0 copy-done.3
  54.1 0.0 copy-done.2
  54.1 103.6 %conditional.1 = (f32[8,1024]{1,0:T(8,128)S(1)}, f32[4096]{0:T(1024)S(1)}, f32[1024]{0:T(1024)S(1)}) conditional(s32[]{:T(128)} %bitcast.8, (f32[32,128]{1,0:T(8,128)S(1)}, f32[8,128]{1,0:T(8,128)S(1)}, f32[8,1024]{1,0:T(8,128)S(1)}) %tuple.24, (f32[4096]{0:T(1024)S(1)}, f32[8,128]{1,0:T(8,128)S(1)}, bf16[64,4096]{1,0:T(8,128)(2,1)S(1)}, ...), branch_computations={%region_0.0_spmd, %region_1.0_spmd} | conditional | bytes 24 | solution.py:638
  54.1 103.5 %branch_1_fun.1 = (f32[1,4096]{1,0:T(1,128)S(1)}, f32[1,1024]{1,0:T(1,128)S(1)}, f32[8,1024]{1,0:T(8,128)S(1)}) custom-call(bf16[64,4096]{1,0:T(8,128)(2,1)S(1)} %get-tuple-element.28.xs, bf16[64,1024]{1,0:T(8,128)(2,1)S(1)} %get-tuple-element.29.ys, f32[1,4096]{1,0:T(1,128)S(1)} %bitcast.10, f32[1,1024]{1,0:T(1,128)S(1)} %bitcast.14, ...), custom_call_target="tpu_custom_call" | custom-call | tf_op jit(solution)/shard_map/cond/branch_1_fun/pallas_call | solution.py:560
  157.6 0.6 copy.25
  158.3 0.6 copy.26
  158.9 0.6 copy.27
Async XLA Ops:
  0.6 53.4 %copy-start = (bf16[64,4096]{1,0:T(8,128)(2,1)S(1)}, bf16[64,4096]{1,0:T(8,128)(2,1)}, u32[]{:S(2)}) copy-start(bf16[64,4096]{1,0:T(8,128)(2,1)} %xs_hbm.1) | copy-start | bytes 1572868
  0.6 53.4 %copy-start.1 = (bf16[64,1024]{1,0:T(8,128)(2,1)S(1)}, bf16[64,1024]{1,0:T(8,128)(2,1)}, u32[]{:S(2)}) copy-start(bf16[64,1024]{1,0:T(8,128)(2,1)} %ys_hbm.1) | copy-start | bytes 393220
  0.7 53.4 %copy-start.3 = (s32[16,16]{1,0:T(8,128)S(1)}, s32[16,16]{1,0:T(8,128)}, u32[]{:S(2)}) copy-start(s32[16,16]{1,0:T(8,128)} %allowed_hbm.1) | copy-start | bytes 3076
  53.3 0.7 copy-start.2
